TPU v7x, 128 devices: a whole 4x4x4 slice. The times are simulated.
128 devices in a mesh: ia: 16 (over z, x), ja: 8 (over y, core).
Axes of the slice: x: 4, y: 4, z: 4, core: 2. Of those that a mesh axis runs over, the one named last changes fastest.
Arguments:
- amplitudes: bfloat16 [8, 16, 128, 128, 128], P(None, 'ia', 'ja'), may hold values from -6 to 6
- coefficients: bfloat16 [8, 16, 128, 128, 128], P(None, 'ia', 'ja'), may hold values from -0.5 to 0.5
- integrals: bfloat16 [8, 16, 128, 128, 128], P(None, 'ia', 'ja'), may hold values from -6 to 6
- pno_energy: float32 [8, 16, 128, 128], P(None, 'ia', 'ja'), may hold values from 0.5 to 4
- pno_counts: int32 [8, 16, 128], P(None, 'ia', 'ja'), may hold values from 32 to 128
- coupled: int32 [8, 16, 128, 12], P(None, 'ia', 'ja'), may hold values 0 or 1
- occ_fock: float32 [128, 128], replicated, may hold values from -1.5 to 1.5
- occ_energy: float32 [128], replicated, may hold values from -1.5 to -0.3
Outputs:
- amplitudes_next: bfloat16 [8, 16, 128, 128, 128], P(None, 'ia', 'ja')
All inputs are finite; a program needn't handle non-finite values. No bound on the sum of `coupled` on one device may be relied on, other than what follows from the above.
Results may differ from a plain program's by a relative error of at most 0.0051.
Values may be sent and summed in bfloat16 or wider, within the bound.
No kernel may reach another device: no remote copies, remote signals or barrier semaphores. Data moves between devices by JAX's collectives and lax.ppermute only.
A program may use at most 128 MiB of HBM per device.

v0:
```python
import jax
import jax.numpy as jnp
from jax import lax
from jax.sharding import PartitionSpec as P

WIN = 6
ITERS = 2


DAMPING = 0.5


def padded(value, sides, width):
    for axis, dim in sides:
        peers, length = (lax.axis_size(axis), value.shape[dim])
        up = [(i, (i + 1) % peers) for i in range(peers - 1)]
        down = [(j, i) for i, j in up]
        last = lax.slice_in_dim(value, length - width, length, axis=dim)
        initial = lax.slice_in_dim(value, 0, width, axis=dim)
        before = lax.ppermute(last, axis, up)
        after = lax.ppermute(initial, axis, down)
        value = jnp.concatenate([before, value, after], axis=dim)
    return value


def window_shift(slot_index):
    return slot_index - WIN if slot_index < WIN else slot_index - WIN + 1


def fock_band(occ_fock):
    orbitals = occ_fock.shape[0]
    places = jnp.arange(orbitals, dtype=jnp.int32)
    rows_out = []
    for slot_index in range(2 * WIN):
        matches = places[:, None] == places[None, :] + window_shift(slot_index)
        rows_out.append(jnp.sum(jnp.where(matches, occ_fock, jnp.zeros_like(occ_fock)), axis=0))
    return jnp.stack(rows_out, axis=0)


def partner_half(half_resid):
    fragments, _, columns, virtuals, _ = half_resid.shape
    outgoing = jnp.transpose(half_resid, (2, 0, 1, 3, 4)).reshape(
        columns * fragments, 1, virtuals, virtuals
    )
    arrived = lax.all_to_all(outgoing, ("ia", "ja"), split_axis=0, concat_axis=1, tiled=True)
    received = arrived.reshape(columns, fragments, virtuals, virtuals)
    return jnp.transpose(received, (1, 0, 3, 2)).reshape(fragments, 1, columns, virtuals, virtuals)


def on_device(
    amplitudes, coefficients, integrals, pno_energy, pno_counts, coupled, occ_fock, occ_energy
):
    fragments, _, columns, virtuals, _ = amplitudes.shape
    row_dev = lax.axis_index("ia")
    col_dev = lax.axis_index("ja")
    levels = jnp.arange(virtuals, dtype=jnp.int32)
    inside_one = levels < pno_counts[..., None]
    inside = inside_one[..., :, None] & inside_one[..., None, :]
    coupling_band = fock_band(occ_fock)
    local_band = lax.dynamic_slice_in_dim(coupling_band, col_dev * columns, columns, 1)
    weights = coupled.astype(jnp.float32) * jnp.transpose(local_band)[None, None, :, :]
    energy_rows = lax.dynamic_slice_in_dim(occ_energy.reshape(fragments, -1), row_dev, 1, 1)
    energy_cols = lax.dynamic_slice_in_dim(occ_energy, col_dev * columns, columns, 0)
    denominator = (
        pno_energy[..., :, None]
        + pno_energy[..., None, :]
        - energy_rows[:, :, None, None, None]
        - energy_cols[None, None, :, None, None]
    )
    current = jnp.where(inside, amplitudes, jnp.zeros_like(amplitudes))
    for sweep in range(ITERS):
        leading = jnp.einsum(
            "fgjab,fgjbc->fgjac", coefficients, current, preferred_element_type=jnp.float32
        ).astype(jnp.bfloat16)
        back_form = jnp.einsum(
            "fgjac,fgjdc->fgjad", leading, coefficients, preferred_element_type=jnp.float32
        ).astype(jnp.bfloat16)
        extended = padded(back_form, (("ja", 2),), WIN)
        left_quad = jnp.einsum(
            "fgjab,fgjbc->fgjac", current, integrals, preferred_element_type=jnp.float32
        ).astype(jnp.bfloat16)
        quadratic = (
            jnp.einsum("fgjac,fgjcd->fgjad", left_quad, current, preferred_element_type=jnp.float32)
            / virtuals
        )
        window_sum = jnp.zeros(back_form.shape, jnp.float32)
        for slot_index in range(2 * WIN):
            begin_at = WIN + window_shift(slot_index)
            window_sum = (
                window_sum
                + weights[..., slot_index][..., None, None]
                * extended[:, :, begin_at : begin_at + columns]
            )
        window_bf = window_sum.astype(jnp.bfloat16)
        left_proj = jnp.einsum(
            "fgjca,fgjcd->fgjad", coefficients, window_bf, preferred_element_type=jnp.float32
        ).astype(jnp.bfloat16)
        projected = jnp.einsum(
            "fgjad,fgjde->fgjae", left_proj, coefficients, preferred_element_type=jnp.float32
        )
        half_resid = (0.5 * integrals.astype(jnp.float32) + quadratic - projected).astype(
            jnp.bfloat16
        )
        partner = partner_half(half_resid)
        residual = half_resid.astype(jnp.float32) + partner.astype(jnp.float32)
        stepped = (1.0 - DAMPING) * current.astype(jnp.float32) - DAMPING * residual / denominator
        current = jnp.where(inside, stepped, jnp.zeros_like(stepped)).astype(jnp.bfloat16)
    return current


def solution(mesh):
    placed = (
        P(None, "ia", "ja", None, None),
        P(None, "ia", "ja", None, None),
        P(None, "ia", "ja", None, None),
        P(None, "ia", "ja", None),
        P(None, "ia", "ja"),
        P(None, "ia", "ja", None),
        P(),
        P(),
    )
    return jax.shard_map(
        on_device,
        mesh=mesh,
        in_specs=placed,
        out_specs=P(None, "ia", "ja", None, None),
        check_vma=False,
    )
```

profile of v0, /device:TPU:1, one launch (start us, length us, event | category | flops | bytes accessed | tf_op | source)
XLA Modules:
  0.0 326.3 jit_solution(2149262423938859958)
XLA Ops:
  0.0 0.8 iota_compare_fusion.12
  0.8 12.0 %convert_bitcast_fusion.1 = bf16[8,1,16,128,128]{4,3,2,0,1:T(8,128)(2,1)} fusion(bf16[8,1,16,128,128]{4,3,2,1,0:T(8,128)(2,1)} %param.9, bf16[8,1,16,128,128]{4,3,2,1,0:T(8,128)(2,1)} %param.8, pred[8,16,128]{2,1,0:T(8,128)(4,1)S(1)} %iota_compare_fusion.12), kind=kOutput, calls=%fused_computation.124 | convolution fusion | flops 1082130432 | bytes 12599296 | tf_op jit(solution)/shard_map/fgjac,fgjdc->fgjad/dot_general | solution.py:75
  12.7 2.1 fusion.161
  14.9 4.6 %collective-permute-start = (bf16[8,1,6,128,128]{4,3,2,0,1:T(8,128)(2,1)S(1)}, bf16[8,1,6,128,128]{4,3,2,0,1:T(8,128)(2,1)}, u32[]{:S(2)}, u32[]{:S(2)}) collective-permute-start(bf16[8,1,6,128,128]{4,3,2,0,1:T(8,128)(2,1)S(1)} %get-tuple-element.19), channel_id=1, source_target_pairs={{0,1},{1,2},{2,3},{3,4},{4,5},{5,6},{6,7},{8,9},{9,10},{10,11},{11... | collective-permute-start | bytes 4718600 | tf_op jit(solution)/shard_map/ppermute | solution.py:20
  19.5 1.9 collective-permute-start.1
  21.5 0.1 select_reduce_fusion
  21.8 11.6 %fusion.57 = f32[8,16,128,128]{3,2,1,0:T(8,128)} fusion(bf16[8,1,16,128,128]{4,3,2,1,0:T(8,128)(2,1)} %param.10, bf16[8,1,16,128,128]{4,3,2,1,0:T(8,128)(2,1)} %param.8, pred[8,16,128]{2,1,0:T(8,128)(4,1)S(1)} %iota_compare_fusion.12), kind=kOutput, calls=%fused_computation.116 | convolution fusion | flops 1084227584 | bytes 16793600 | tf_op jit(solution)/shard_map/fgjac,fgjcd->fgjad/dot_general | solution.py:83
  33.4 3.4 %collective-permute-done = bf16[8,1,6,128,128]{4,3,2,0,1:T(8,128)(2,1)} collective-permute-done((bf16[8,1,6,128,128]{4,3,2,0,1:T(8,128)(2,1)S(1)}, bf16[8,1,6,128,128]{4,3,2,0,1:T(8,128)(2,1)}, u32[]{:S(2)}, u32[]{:S(2)}) %collective-permute-start) | collective-permute-done | bytes 1572896 | tf_op jit(solution)/shard_map/ppermute | solution.py:20
  36.8 4.5 %collective-permute-done.1 = bf16[8,1,6,128,128]{4,3,2,0,1:T(8,128)(2,1)} collective-permute-done((bf16[8,1,6,128,128]{4,3,2,0,1:T(8,128)(2,1)S(1)}, bf16[8,1,6,128,128]{4,3,2,0,1:T(8,128)(2,1)}, u32[]{:S(2)}, u32[]{:S(2)}) %collective-permute-start.1) | collective-permute-done | bytes 1572896 | tf_op jit(solution)/shard_map/ppermute | solution.py:21
  41.3 36.3 %fusion.9 = bf16[8,1,16,128,128]{4,3,2,0,1:T(8,128)(2,1)} fusion(f32[8,16,128,128]{3,2,1,0:T(8,128)} %fusion.57, bf16[8,1,16,128,128]{4,3,2,1,0:T(8,128)(2,1)} %param.10, bf16[8,1,16,128,128]{4,3,2,1,0:T(8,128)(2,1)} %param.9, bf16[8,1,6,128,128]{4,3,2,0,1:T(8,128)(2,1)} %collective-permute-done.1, bf16[8,1,16,128,128]{4,3,2,0,1:T(8,128)(2,1)} %convert_bitcast_fusion.1, ...), kind=kOutput, calls=%fused_computation.37 | convolution fusion | flops 1189085184 | bytes 32512000 | tf_op jit(solution)/shard_map/fgjad,fgjde->fgjae/dot_general | solution.py:98
  77.6 4.8 %copy.28 = bf16[16,8,1,128,128]{4,3,1,0,2:T(8,128)(2,1)} copy(bf16[16,8,1,128,128]{4,3,0,1,2:T(8,128)(2,1)} %bitcast.250) | data formatting | bytes 8388608 | tf_op jit(solution)/shard_map/transpose | solution.py:42
  82.4 10.3 %all-to-all-start = ((bf16[128,1,128,128]{3,2,1,0:T(8,128)(2,1)}), bf16[128,1,128,128]{3,2,1,0:T(8,128)(2,1)}, u32[]{:S(2)}, u32[]{:S(2)}) async-start(bf16[128,1,128,128]{3,2,1,0:T(8,128)(2,1)} %bitcast.248), calls=%async_computation | async-start | bytes 8388608 | tf_op jit(solution)/shard_map/all_to_all | solution.py:45
  92.7 0.1 dynamic_slice.11
  92.8 0.1 reshape.240
  92.9 0.2 dynamic-slice_reduce_fusion
  93.1 52.4 %all-to-all-done = bf16[128,1,128,128]{3,2,1,0:T(8,128)(2,1)} async-done(((bf16[128,1,128,128]{3,2,1,0:T(8,128)(2,1)}), bf16[128,1,128,128]{3,2,1,0:T(8,128)(2,1)}, u32[]{:S(2)}, u32[]{:S(2)}) %all-to-all-start) | async-done | bytes 4194336 | tf_op jit(solution)/shard_map/all_to_all | solution.py:45
  145.5 6.5 %bitcast_convert_fusion.1 = f32[16,8,128,128]{3,2,1,0:T(8,128)} fusion(bf16[16,8,128,128]{3,2,1,0:T(8,128)(2,1)} %bitcast.246), kind=kLoop, calls=%fused_computation.88 | loop fusion | flops 2097152 | bytes 12582912 | tf_op jit(solution)/shard_map/convert_element_type | solution.py:105
  152.0 9.2 %copy.31 = f32[16,8,128,128]{2,3,0,1:T(8,128)} copy(f32[16,8,128,128]{3,2,1,0:T(8,128)} %bitcast_convert_fusion.1) | data formatting | bytes 16777216 | tf_op jit(solution)/shard_map/convert_element_type | solution.py:105
  161.2 10.0 %fusion = bf16[8,1,16,128,128]{4,3,2,0,1:T(8,128)(2,1)} fusion(f32[16,8,128,128]{2,3,0,1:T(8,128)} %copy.31, bf16[8,1,16,128,128]{4,3,2,0,1:T(8,128)(2,1)} %fusion.9, f32[16]{0:T(128)S(1)} %dynamic_slice.11, f32[8]{0:T(128)S(1)} %dynamic-slice_reduce_fusion, f32[8,16,128]{2,1,0:T(8,128)S(1)} %bitcast.252, pred[8,16,128]{2,1,0:T(8,128)(4,1)S(1)} %iota_compare_fusion.12, ...), kind=kLoop, calls=%fused_computation.23 | loop fusion | flops 29360128 | bytes 21053536 | tf_op jit(solution)/shard_map/convert_element_type | solution.py:107
  171.2 11.5 %convert_bitcast_fusion = bf16[8,1,16,128,128]{4,3,2,0,1:T(8,128)(2,1)} fusion(bf16[8,1,16,128,128]{4,3,2,1,0:T(8,128)(2,1)} %param.9, bf16[8,1,16,128,128]{4,3,2,0,1:T(8,128)(2,1)} %fusion), kind=kOutput, calls=%fused_computation.120 | convolution fusion | flops 1077936128 | bytes 12582912 | tf_op jit(solution)/shard_map/fgjac,fgjdc->fgjad/dot_general | solution.py:75
  182.7 2.1 fusion.160
  184.8 2.8 collective-permute-start.2
  187.7 2.6 collective-permute-start.3
  190.3 10.3 %fusion.34 = f32[8,16,128,128]{3,2,1,0:T(8,128)} fusion(bf16[8,1,16,128,128]{4,3,2,0,1:T(8,128)(2,1)} %fusion, bf16[8,1,16,128,128]{4,3,2,1,0:T(8,128)(2,1)} %param.10), kind=kOutput, calls=%fused_computation.93 | convolution fusion | flops 1075838976 | bytes 16777216 | tf_op jit(solution)/shard_map/fgjac,fgjcd->fgjad/dot_general | solution.py:83
  200.6 4.4 %collective-permute-done.2 = bf16[8,1,6,128,128]{4,3,2,0,1:T(8,128)(2,1)} collective-permute-done((bf16[8,1,6,128,128]{4,3,2,0,1:T(8,128)(2,1)S(1)}, bf16[8,1,6,128,128]{4,3,2,0,1:T(8,128)(2,1)}, u32[]{:S(2)}, u32[]{:S(2)}) %collective-permute-start.2) | collective-permute-done | bytes 1572896 | tf_op jit(solution)/shard_map/ppermute | solution.py:20
  205.0 4.5 %collective-permute-done.3 = bf16[8,1,6,128,128]{4,3,2,0,1:T(8,128)(2,1)} collective-permute-done((bf16[8,1,6,128,128]{4,3,2,0,1:T(8,128)(2,1)S(1)}, bf16[8,1,6,128,128]{4,3,2,0,1:T(8,128)(2,1)}, u32[]{:S(2)}, u32[]{:S(2)}) %collective-permute-start.3) | collective-permute-done | bytes 1572896 | tf_op jit(solution)/shard_map/ppermute | solution.py:21
  209.5 35.5 %fusion.8 = bf16[8,1,16,128,128]{4,3,2,0,1:T(8,128)(2,1)} fusion(f32[8,16,128,128]{3,2,1,0:T(8,128)} %fusion.34, bf16[8,1,16,128,128]{4,3,2,1,0:T(8,128)(2,1)} %param.10, bf16[8,1,16,128,128]{4,3,2,1,0:T(8,128)(2,1)} %param.9, bf16[8,1,6,128,128]{4,3,2,0,1:T(8,128)(2,1)} %collective-permute-done.3, bf16[8,1,16,128,128]{4,3,2,0,1:T(8,128)(2,1)} %convert_bitcast_fusion, ...), kind=kOutput, calls=%fused_computation.34 | convolution fusion | flops 1189085184 | bytes 32512000 | tf_op jit(solution)/shard_map/fgjad,fgjde->fgjae/dot_general | solution.py:98
  245.0 2.5 copy.36
  247.5 56.7 %all_to_all.8 = bf16[128,1,128,128]{3,2,1,0:T(8,128)(2,1)S(1)} all-to-all(bf16[128,1,128,128]{3,2,1,0:T(8,128)(2,1)S(1)} %bitcast.249), channel_id=1, replica_groups=mesh['ia'=16,'ja'=8] {'ia','ja'}, dimensions={0} | all-to-all | bytes 8388608 | tf_op jit(solution)/shard_map/all_to_all | solution.py:45
  304.3 4.3 %bitcast_convert_fusion = f32[16,8,128,128]{3,2,1,0:T(8,128)} fusion(bf16[16,8,128,128]{3,2,1,0:T(8,128)(2,1)S(1)} %bitcast.247), kind=kLoop, calls=%fused_computation.87 | loop fusion | flops 2097152 | bytes 12582912 | tf_op jit(solution)/shard_map/convert_element_type | solution.py:105
  308.5 9.1 %copy.39 = f32[16,8,128,128]{2,3,0,1:T(8,128)} copy(f32[16,8,128,128]{3,2,1,0:T(8,128)} %bitcast_convert_fusion) | data formatting | bytes 16777216 | tf_op jit(solution)/shard_map/convert_element_type | solution.py:105
  317.6 8.5 %fusion.66 = bf16[8,1,16,128,128]{4,3,2,1,0:T(8,128)(2,1)} fusion(f32[16]{0:T(128)S(1)} %dynamic_slice.11, f32[8]{0:T(128)S(1)} %dynamic-slice_reduce_fusion, f32[8,16,128]{2,1,0:T(8,128)S(1)} %bitcast.253, f32[16,8,128,128]{2,3,0,1:T(8,128)} %copy.39, bf16[8,1,16,128,128]{4,3,2,0,1:T(8,128)(2,1)} %fusion.8, bf16[8,1,16,128,128]{4,3,2,0,1:T(8,128)(2,1)} %fusion, ...), kind=kLoop, calls=%fused_computation.127 | loop fusion | flops 27262976 | bytes 21053536 | tf_op jit(solution)/shard_map/convert_element_type | solution.py:107
  (18 shorter events, 0.2 us)
Async XLA Ops:
  12.7 8.7 %copy-start.1 = (f32[128,128]{1,0:T(8,128)S(1)}, f32[128,128]{1,0:T(8,128)}, u32[]{:S(2)}) copy-start(f32[128,128]{1,0:T(8,128)} %param.14) | copy-start | bytes 196612
  12.7 9.0 %copy-start.2 = (s32[8,1,16,12]{2,1,3,0:T(1,128)S(1)}, s32[8,1,16,12]{2,1,3,0:T(1,128)}, u32[]{:S(2)}) copy-start(s32[8,1,16,12]{2,1,3,0:T(1,128)} %param.13) | copy-start | bytes 18436
  14.9 21.9 %collective-permute-start = (bf16[8,1,6,128,128]{4,3,2,0,1:T(8,128)(2,1)S(1)}, bf16[8,1,6,128,128]{4,3,2,0,1:T(8,128)(2,1)}, u32[]{:S(2)}, u32[]{:S(2)}) collective-permute-start(bf16[8,1,6,128,128]{4,3,2,0,1:T(8,128)(2,1)S(1)} %get-tuple-element.19), channel_id=1, source_target_pairs={{0,1},{1,2},{2,3},{3,4},{4,5},{5,6},{6,7},{8,9},{9,10},{10,11},{11... | collective-permute-start | bytes 4718600 | tf_op jit(solution)/shard_map/ppermute | solution.py:20
  19.5 21.8 %collective-permute-start.1 = (bf16[8,1,6,128,128]{4,3,2,0,1:T(8,128)(2,1)S(1)}, bf16[8,1,6,128,128]{4,3,2,0,1:T(8,128)(2,1)}, u32[]{:S(2)}, u32[]{:S(2)}) collective-permute-start(bf16[8,1,6,128,128]{4,3,2,0,1:T(8,128)(2,1)S(1)} %get-tuple-element.20), channel_id=1, source_target_pairs={{1,0},{2,1},{3,2},{4,3},{5,4},{6,5},{7,6},{9,8},{10,9},{11,10},{12... | collective-permute-start | bytes 4718600 | tf_op jit(solution)/shard_map/ppermute | solution.py:21
  82.4 10.3 %copy-start.3 = (f32[128]{0:T(128)S(1)}, f32[128]{0:T(128)}, u32[]{:S(2)}) copy-start(f32[128]{0:T(128)} %param.15) | copy-start | bytes 1540
  82.4 63.1 %all-to-all-start = ((bf16[128,1,128,128]{3,2,1,0:T(8,128)(2,1)}), bf16[128,1,128,128]{3,2,1,0:T(8,128)(2,1)}, u32[]{:S(2)}, u32[]{:S(2)}) async-start(bf16[128,1,128,128]{3,2,1,0:T(8,128)(2,1)} %bitcast.248), calls=%async_computation | async-start | bytes 8388608 | tf_op jit(solution)/shard_map/all_to_all | solution.py:45
  152.0 9.2 %copy-start = (f32[8,1,16,128]{3,2,1,0:T(8,128)S(1)}, f32[8,1,16,128]{3,2,1,0:T(8,128)}, u32[]{:S(2)}) copy-start(f32[8,1,16,128]{3,2,1,0:T(8,128)} %param.11) | copy-start | bytes 196612
  184.8 20.2 %collective-permute-start.2 = (bf16[8,1,6,128,128]{4,3,2,0,1:T(8,128)(2,1)S(1)}, bf16[8,1,6,128,128]{4,3,2,0,1:T(8,128)(2,1)}, u32[]{:S(2)}, u32[]{:S(2)}) collective-permute-start(bf16[8,1,6,128,128]{4,3,2,0,1:T(8,128)(2,1)S(1)} %get-tuple-element.17), channel_id=1, source_target_pairs={{0,1},{1,2},{2,3},{3,4},{4,5},{5,6},{6,7},{8,9},{9,10},{10,11},{11... | collective-permute-start | bytes 4718600 | tf_op jit(solution)/shard_map/ppermute | solution.py:20
  187.7 21.8 %collective-permute-start.3 = (bf16[8,1,6,128,128]{4,3,2,0,1:T(8,128)(2,1)S(1)}, bf16[8,1,6,128,128]{4,3,2,0,1:T(8,128)(2,1)}, u32[]{:S(2)}, u32[]{:S(2)}) collective-permute-start(bf16[8,1,6,128,128]{4,3,2,0,1:T(8,128)(2,1)S(1)} %get-tuple-element.18), channel_id=1, source_target_pairs={{1,0},{2,1},{3,2},{4,3},{5,4},{6,5},{7,6},{9,8},{10,9},{11,10},{12... | collective-permute-start | bytes 4718600 | tf_op jit(solution)/shard_map/ppermute | solution.py:21
where the time goes:
time: 327 us; the launch traced here: 326 us
  matrix products  117 us (36%)
  waiting for transfers between devices  69.3 us (21%)
  blocking collectives  56.7 us (17%)
  local copies, waits for them, and re-layouts  30.3 us (9%)
  other arithmetic  30.2 us (9%)
  starting transfers between devices  22.3 us (7%)
    dot_general x2, matrix products, on_device(): jnp.einsum('fgjad,fgjde->fgjae', left_proj, coefficients, preferred_eleme...  71.8 us
    all_to_all x1, blocking collectives, partner_half(): lax.all_to_all(outgoing, ('ia', 'ja'), split_axis=0, concat_axis=1, tiled...  56.7 us
    all_to_all x1, waiting for transfers between devices, partner_half(): lax.all_to_all(outgoing, ('ia', 'ja'), split_axis=0, concat_axis=1, tiled...  52.4 us
    dot_general x2, matrix products, on_device(): jnp.einsum('fgjac,fgjdc->fgjad', leading, coefficients, preferred_element...  23.4 us
    dot_general x2, matrix products, on_device(): jnp.einsum('fgjac,fgjcd->fgjad', left_quad, current, preferred_element_ty...  21.9 us
    convert_element_type x2, other arithmetic, on_device(): jnp.where(inside, stepped, jnp.zeros_like(stepped)).astype(jnp.bfloat16)  18.5 us
    convert_element_type x2, local copies, waits for them, and re-layouts, on_device(): residual = half_resid.astype(jnp.float32) + partner.astype(jnp.float32)  18.3 us
    convert_element_type x2, other arithmetic, on_device(): residual = half_resid.astype(jnp.float32) + partner.astype(jnp.float32)  10.7 us
  transfers between devices with their start and end apart: 5, of which 5 were waited for; matrix products, arithmetic and copies ran while one was open for 7% of the time, Pallas kernels for 0%

commit v1 on v0

v1 whole, which is shorter than its diff:
```python
from functools import partial

import jax
import jax.numpy as jnp
from jax import lax
from jax.experimental import pallas as pl
from jax.experimental.pallas import tpu as pltpu
from jax.sharding import PartitionSpec as P

WIN = 6
ITERS = 2
DAMPING = 0.5
GROUPS = 2
SKEW = 4
VMEM_BYTES = 16 * 1024 * 1024

BF = jnp.bfloat16
F32 = jnp.float32


def window_shift(slot_index):
    return slot_index - WIN if slot_index < WIN else slot_index - WIN + 1


def nn(a, b):
    return lax.dot_general(a, b, (((1,), (0,)), ((), ())), preferred_element_type=F32)


def nt(a, b):
    return lax.dot_general(a, b, (((1,), (1,)), ((), ())), preferred_element_type=F32)


def tn(a, b):
    return lax.dot_general(a, b, (((0,), (0,)), ((), ())), preferred_element_type=F32)


def inside_mask(count, virtuals):
    rows = lax.broadcasted_iota(jnp.int32, (virtuals, virtuals), 0)
    cols = lax.broadcasted_iota(jnp.int32, (virtuals, virtuals), 1)
    return jnp.maximum(rows, cols) < count


def back_forms(f, amps, coef, x_ref, first_ref, last_ref):
    columns = x_ref.shape[1]
    ready, leading = {}, {}
    for step in range(columns + 2 * SKEW):
        b = step
        if b < columns:
            ready[b] = amps(b)
        b = step - SKEW
        if 0 <= b < columns:
            leading[b] = nn(coef(b), ready.pop(b)).astype(BF)
        b = step - 2 * SKEW
        if 0 <= b:
            back = nt(leading.pop(b), coef(b)).astype(BF)
            x_ref[f, b] = back
            if b < WIN:
                first_ref[f, b] = back
            if b >= columns - WIN:
                last_ref[f, b - (columns - WIN)] = back


def masked_forms(f, offset, counts_ref, raw_ref, c_ref, tm_ref, x_ref, first_ref, last_ref):
    virtuals = x_ref.shape[2]

    def amps(b):
        keep = inside_mask(counts_ref[f + offset, b], virtuals)
        value = jnp.where(keep, raw_ref[f, b].astype(F32), 0.0).astype(BF)
        tm_ref[f, b] = value
        return value

    back_forms(f, amps, lambda b: c_ref[f, b], x_ref, first_ref, last_ref)


def start_kernel(
    counts_ref, t_hbm, c_hbm, tm_ref, c_ref, raw_next, c_next, x_ref, first_ref, last_ref,
    raw_ref, sems, next_sems,
):
    size = x_ref.shape[0]

    def loads(f):
        return (
            pltpu.make_async_copy(t_hbm.at[f, 0], raw_ref.at[f], sems.at[f, 0]),
            pltpu.make_async_copy(c_hbm.at[f, 0], c_ref.at[f], sems.at[f, 1]),
        )

    for f in range(size):
        for load in loads(f):
            load.start()
    rest = pl.ds(size, size)
    later = (
        pltpu.make_async_copy(t_hbm.at[rest, 0], raw_next, next_sems.at[0]),
        pltpu.make_async_copy(c_hbm.at[rest, 0], c_next, next_sems.at[1]),
    )
    for load in later:
        load.start()

    def body(f, carry):
        for load in loads(f):
            load.wait()
        masked_forms(f, 0, counts_ref, raw_ref, c_ref, tm_ref, x_ref, first_ref, last_ref)
        return carry

    lax.fori_loop(0, size, body, 0)
    for load in later:
        load.wait()


def second_kernel(
    counts_ref, raw_ref, c_ref, k_hbm, tm_ref, k_ref, x_ref, first_ref, last_ref, sems
):
    size = x_ref.shape[0]
    load = pltpu.make_async_copy(k_hbm.at[:, 0], k_ref, sems.at[0])
    load.start()

    def body(f, carry):
        masked_forms(f, size, counts_ref, raw_ref, c_ref, tm_ref, x_ref, first_ref, last_ref)
        return carry

    lax.fori_loop(0, size, body, 0)
    load.wait()


def updated(f, b, offset, idx_ref, occ_ref, counts_ref, rows_energy, e_ref, h_ref, p_ref, t_ref):
    columns, virtuals = t_ref.shape[1:3]
    occ_row = occ_ref[(f + offset) * columns + idx_ref[0]]
    occ_col = occ_ref[idx_ref[1] * columns + b]
    cols_energy = e_ref[f + offset, 0, b : b + 1, :]
    denominator = (rows_energy[:, b : b + 1] - occ_row) + (cols_energy - occ_col)
    inverse = pl.reciprocal(denominator)
    residual = h_ref[b, f + offset].astype(F32) + p_ref[b, f + offset].T.astype(F32)
    stepped = (1.0 - DAMPING) * t_ref[f, b].astype(F32) - (DAMPING * residual) * inverse
    keep = inside_mask(counts_ref[f + offset, b], virtuals)
    return jnp.where(keep, stepped, 0.0).astype(BF)


def middle_kernel(
    offset, idx_ref, occ_ref, counts_ref, e_ref, h_ref, p_ref, t_ref, c_ref,
    tm_ref, x_ref, first_ref, last_ref,
):
    def body(f, carry):
        rows_energy = e_ref[f + offset, 0].T

        def amps(b):
            value = updated(
                f, b, offset, idx_ref, occ_ref, counts_ref, rows_energy, e_ref, h_ref, p_ref, t_ref
            )
            tm_ref[f, b] = value
            return value

        back_forms(f, amps, lambda b: c_ref[f, b], x_ref, first_ref, last_ref)
        return carry

    lax.fori_loop(0, x_ref.shape[0], body, 0)


def last_kernel(idx_ref, occ_ref, counts_ref, e_ref, h_ref, p_ref, *rest):
    out_hbm, made_ref, sems = rest[-3:]
    t_refs = rest[:-3]
    size, columns = t_refs[0].shape[:2]

    def store(f):
        return pltpu.make_async_copy(made_ref.at[f], out_hbm.at[f, 0], sems.at[f])

    for g, t_ref in enumerate(t_refs):
        offset = g * size

        def body(f, carry, offset=offset, t_ref=t_ref):
            rows_energy = e_ref[f + offset, 0].T
            for b in range(columns):
                made_ref[f + offset, b] = updated(
                    f, b, offset, idx_ref, occ_ref, counts_ref, rows_energy, e_ref, h_ref, p_ref, t_ref
                )
            store(f + offset).start()
            return carry

        lax.fori_loop(0, size, body, 0)
    for f in range(len(t_refs) * size):
        store(f).wait()


def half_kernel(offset, w_ref, t_ref, c_ref, k_ref, x_ref, before_ref, after_ref, *rest):
    h_ref, xf = rest[-2:]
    size, columns, virtuals = x_ref.shape[:3]
    lag = columns // 2

    def body(f, carry):
        xf[0:WIN] = before_ref[f].astype(F32)
        xf[WIN : WIN + columns] = x_ref[f].astype(F32)
        xf[WIN + columns : 2 * WIN + columns] = after_ref[f].astype(F32)
        window, left_proj, left_quad = {}, {}, {}
        for step in range(columns + 2 * lag):
            b = step
            if b < columns:
                total = w_ref[f + offset, b * 2 * WIN] * xf[b + WIN + window_shift(0)]
                for s in range(1, 2 * WIN):
                    total = total + w_ref[f + offset, b * 2 * WIN + s] * xf[b + WIN + window_shift(s)]
                window[b] = total.astype(BF)
            b = step - lag
            if 0 <= b < columns:
                left_proj[b] = tn(c_ref[f, b], window.pop(b)).astype(BF)
                left_quad[b] = (nn(t_ref[f, b], k_ref[f + offset, b]) * (1.0 / virtuals)).astype(BF)
            b = step - 2 * lag
            if 0 <= b:
                joined = nn(
                    jnp.concatenate([left_quad.pop(b), -left_proj.pop(b)], axis=1),
                    jnp.concatenate([t_ref[f, b], c_ref[f, b]], axis=0),
                )
                h_ref[b, f + offset] = (0.5 * k_ref[f + offset, b].astype(F32) + joined).astype(BF)
        return carry

    lax.fori_loop(0, size, body, 0)


SMEM = pl.BlockSpec(memory_space=pltpu.SMEM)
VMEM = pl.BlockSpec(memory_space=pltpu.VMEM)
HBM = pl.BlockSpec(memory_space=pltpu.HBM)


def params():
    return pltpu.CompilerParams(vmem_limit_bytes=VMEM_BYTES)


def near_core(value):
    return pltpu.with_memory_space_constraint(value, pltpu.VMEM)


def far(value):
    return pltpu.with_memory_space_constraint(value, pltpu.HBM)


def cost(flops, moved):
    return pl.CostEstimate(flops=flops, bytes_accessed=moved, transcendentals=0)


def on_device(
    amplitudes, coefficients, integrals, pno_energy, pno_counts, coupled, occ_fock, occ_energy
):
    fragments, _, columns, virtuals, _ = amplitudes.shape
    size = fragments // GROUPS
    pairs = size * columns
    matmul = 2 * virtuals**3 * pairs
    block = 2 * virtuals**2 * pairs
    col_dev = lax.axis_index("ja")
    idx = jnp.stack([lax.axis_index("ia"), col_dev]).astype(jnp.int32)
    counts = pno_counts.reshape(fragments, columns)
    near = lax.dynamic_slice(
        jnp.pad(occ_fock, ((WIN, WIN), (0, 0))),
        (col_dev * columns, col_dev * columns),
        (columns + 2 * WIN, columns),
    )
    reach = jnp.arange(columns + 2 * WIN)[None, None, :]
    place = jnp.arange(columns)[:, None, None]
    shifts = jnp.array([window_shift(s) + WIN for s in range(2 * WIN)])[None, :, None]
    band = jnp.sum(jnp.where(reach == place + shifts, jnp.transpose(near)[:, None, :], 0.0), axis=2)
    weights = (coupled.astype(F32) * band[None, None]).reshape(fragments, columns * 2 * WIN)
    weights, idx, counts, amplitudes = lax.optimization_barrier((weights, idx, counts, amplitudes))
    energies = near_core(pno_energy)

    peers = lax.axis_size("ja")
    up = [(i, i + 1) for i in range(peers - 1)]
    down = [(j, i) for i, j in up]

    def near_shape(*lead):
        return pltpu.VMEM((*lead, virtuals, virtuals), BF)

    group = near_shape(size, columns)
    back = [group, near_shape(size, WIN), near_shape(size, WIN)]

    def first_steps():
        tm, c, raw_next, c_next, *made = pl.pallas_call(
            start_kernel,
            in_specs=[SMEM, HBM, HBM],
            out_shape=[group] * 4 + back,
            out_specs=[VMEM] * 7,
            scratch_shapes=[
                pltpu.VMEM((size, columns, virtuals, virtuals), BF),
                pltpu.SemaphoreType.DMA((size, 2)),
                pltpu.SemaphoreType.DMA((2,)),
            ],
            compiler_params=params(),
            cost_estimate=cost(2 * matmul, 4 * block),
            name="start",
        )(counts, far(amplitudes), far(coefficients))
        borders = [exchange(made)]
        tm_next, k, *made_next = pl.pallas_call(
            second_kernel,
            in_specs=[SMEM, VMEM, VMEM, HBM],
            out_shape=[group, near_shape(fragments, columns)] + back,
            out_specs=[VMEM] * 5,
            scratch_shapes=[pltpu.SemaphoreType.DMA((1,))],
            compiler_params=params(),
            cost_estimate=cost(2 * matmul, 2 * block),
            name="second",
        )(counts, near_core(raw_next), near_core(c_next), far(integrals))
        borders.append(exchange(made_next))
        return [tm, tm_next], [c, c_next], k, [made[0], made_next[0]], borders

    def exchange(made):
        return lax.ppermute(made[2], "ja", up), lax.ppermute(made[1], "ja", down)

    def next_step(g, halves, partner, current, coefs):
        return pl.pallas_call(
            partial(middle_kernel, g * size),
            in_specs=[SMEM] * 3 + [VMEM] * 5,
            out_shape=[group] + back,
            out_specs=[VMEM] * 4,
            compiler_params=params(),
            cost_estimate=cost(2 * matmul, block),
            name="middle",
        )(
            idx, occ_energy, counts, energies, near_core(halves), near_core(partner),
            near_core(current[g]), near_core(coefs[g]),
        )

    def half_step(g, current, coefs, ints, back_form, before, after, out):
        operands = [current[g], coefs[g], ints, back_form, before, after]
        aliases = {}
        if out is not None:
            aliases = {len(operands) + 1: 0}
            operands.append(out)
        return pl.pallas_call(
            partial(half_kernel, g * size),
            in_specs=[SMEM] + [VMEM] * len(operands),
            out_shape=near_shape(columns, fragments),
            out_specs=VMEM,
            scratch_shapes=[pltpu.VMEM((columns + 2 * WIN, virtuals, virtuals), F32)],
            input_output_aliases=aliases,
            compiler_params=params(),
            cost_estimate=cost(4 * matmul, 2 * block),
            name="half",
        )(weights, *map(near_core, operands))

    def last_step(halves, partner, current):
        return pl.pallas_call(
            last_kernel,
            in_specs=[SMEM] * 3 + [VMEM] * (3 + GROUPS),
            out_shape=pltpu.HBM(amplitudes.shape, BF),
            out_specs=HBM,
            scratch_shapes=[
                pltpu.VMEM((fragments, columns, virtuals, virtuals), BF),
                pltpu.SemaphoreType.DMA((fragments,)),
            ],
            compiler_params=params(),
            cost_estimate=cost(0, 2 * GROUPS * block),
            name="last",
        )(
            idx, occ_energy, counts, energies, near_core(halves), near_core(partner),
            *map(near_core, current),
        )

    halves = partner = None
    for sweep in range(ITERS):
        if sweep == 0:
            current, coefs, ints, back_form, borders = first_steps()
        else:
            new, back_form, borders = [], [], []
            for g in range(GROUPS):
                tm, *made = next_step(g, halves, partner, current, coefs)
                borders.append(exchange(made))
                new.append(tm)
                back_form.append(made[0])
            current = new
        halves = None
        for g in range(GROUPS):
            halves = half_step(g, current, coefs, ints, back_form[g], *borders[g], halves)
        sent = halves.reshape(columns * fragments, 1, virtuals, virtuals)
        arrived = lax.all_to_all(sent, ("ia", "ja"), split_axis=0, concat_axis=0, tiled=True)
        partner = arrived.reshape(columns, fragments, virtuals, virtuals)
    return last_step(halves, partner, current)


def solution(mesh):
    placed = (
        P(None, "ia", "ja", None, None),
        P(None, "ia", "ja", None, None),
        P(None, "ia", "ja", None, None),
        P(None, "ia", "ja", None),
        P(None, "ia", "ja"),
        P(None, "ia", "ja", None),
        P(),
        P(),
    )
    return jax.shard_map(
        on_device,
        mesh=mesh,
        in_specs=placed,
        out_specs=P(None, "ia", "ja", None, None),
        check_vma=False,
    )
```

time: 327 us -> 206 us (0.63)
  matrix products: 117 us -> 0 us
  blocking collectives: 56.7 us -> 119 us
  waiting for transfers between devices: 69.3 us -> 9.32 us
  Pallas kernels: 0 us -> 51.1 us
  local copies, waits for them, and re-layouts: 30.3 us -> 1.81 us
  other arithmetic: 30.2 us -> 1.82 us
    dot_general x6 -> x0, matrix products: 117 us -> none  [the longest x2 71.8 us: on_device(): jnp.einsum('fgjad,fgjde->fgjae', left_proj, coefficients, preferred_eleme...]
    all_to_all x1 -> x2, blocking collectives: 56.7 us -> 119 us  [on_device(): lax.all_to_all(sent, ('ia', 'ja'), split_axis=0, concat_axis=0, tiled=True)]
    all_to_all x1 -> x0, waiting for transfers between devices: 52.4 us -> none  [partner_half(): lax.all_to_all(outgoing, ('ia', 'ja'), split_axis=0, concat_axis=1, tiled...]
    pallas_call x0 -> x9, Pallas kernels: none -> 51.1 us  [the longest x4 26.9 us: half_step(): pl.pallas_call(partial(half_kernel, g * size), in_specs=[SMEM] + [VMEM] *...]
    convert_element_type x4 -> x0, other arithmetic: 29.3 us -> none  [the longest x2 18.5 us: on_device(): jnp.where(inside, stepped, jnp.zeros_like(stepped)).astype(jnp.bfloat16)]
    convert_element_type x2 -> x0, local copies, waits for them, and re-layouts: 18.3 us -> none  [on_device(): residual = half_resid.astype(jnp.float32) + partner.astype(jnp.float32)]
    ppermute x4 -> x8, starting transfers between devices: 12 us -> 22.4 us  [exchange(): return (lax.ppermute(made[2], 'ja', up), lax.ppermute(made[1], 'ja', down))]
    all_to_all x1 -> x0, starting transfers between devices: 10.3 us -> none  [partner_half(): lax.all_to_all(outgoing, ('ia', 'ja'), split_axis=0, concat_axis=1, tiled...]
  transfers between devices with their start and end apart: 5 -> 8, of which waited for: 5 -> 4; matrix products, arithmetic and copies ran while one was open for 7% -> 0% of each run, Pallas kernels for 0% -> 10%
where the time goes in v1:
time: 206 us
  blocking collectives  119 us (58%)
  Pallas kernels  51.1 us (25%)
  starting transfers between devices  22.4 us (11%)
  waiting for transfers between devices  9.32 us (5%)
    all_to_all x2, blocking collectives, on_device(): lax.all_to_all(sent, ('ia', 'ja'), split_axis=0, concat_axis=0, tiled=True)  119 us
    pallas_call x4, Pallas kernels, half_step(): pl.pallas_call(partial(half_kernel, g * size), in_specs=[SMEM] + [VMEM] *...  26.9 us
    ppermute x8, starting transfers between devices, exchange(): return (lax.ppermute(made[2], 'ja', up), lax.ppermute(made[1], 'ja', down))  22.4 us
    ppermute x8, waiting for transfers between devices, exchange(): return (lax.ppermute(made[2], 'ja', up), lax.ppermute(made[1], 'ja', down))  9.32 us
    pallas_call x2, Pallas kernels, next_step(): pl.pallas_call(partial(middle_kernel, g * size), in_specs=[SMEM] * 3 + [V...  9.21 us
    pallas_call x1, Pallas kernels, last_step(): pl.pallas_call(last_kernel, in_specs=[SMEM] * 3 + [VMEM] * (3 + GROUPS),...  7.08 us
    pallas_call x1, Pallas kernels, first_steps(): pl.pallas_call(start_kernel, in_specs=[SMEM, HBM, HBM], out_shape=[group]...  4.58 us
  transfers between devices with their start and end apart: 8, of which 4 were waited for; matrix products, arithmetic and copies ran while one was open for 0% of the time, Pallas kernels for 10%

profile of v1, /device:TPU:1, one launch (start us, length us, event | category | flops | bytes accessed | tf_op | source)
XLA Modules:
  0.0 205.9 jit_solution(6022554341745993407)
XLA Ops:
  0.0 0.8 fusion
  0.8 0.1 copy.20
  0.9 0.7 iota_add_fusion
  1.6 0.2 select_reduce_fusion
  1.8 0.8 convert_multiply_fusion
  2.6 0.1 copy.21
  2.8 0.1 reshape.44.w_ref
  2.9 0.1 pad_add_fusion.idx_ref
  2.9 0.7 copy-done.1
  3.6 4.6 %start.1 = (bf16[4,16,128,128]{3,2,1,0:T(8,128)(2,1)S(1)}, bf16[4,16,128,128]{3,2,1,0:T(8,128)(2,1)S(1)}, bf16[4,16,128,128]{3,2,1,0:T(8,128)(2,1)S(1)}, bf16[4,...) custom-call(s32[8,16]{1,0:T(8,128)S(1)} %bitcast.22, ...), custom_call_target="tpu_custom_call" | custom-call | flops 536870912 | bytes 8388608 | tf_op jit(solution)/shard_map/start/pallas_call | solution.py:271
  8.2 4.6 %collective-permute-start.2 = (bf16[4,6,128,128]{3,2,1,0:T(8,128)(2,1)S(1)}, bf16[4,6,128,128]{3,2,1,0:T(8,128)(2,1)S(1)}, u32[]{:S(2)}, u32[]{:S(2)}) collective-permute-start(bf16[4,6,128,128]{3,2,1,0:T(8,128)(2,1)S(1)} %get-tuple-element.43), channel_id=1, source_target_pairs={{0,1},{1,2},{2,3},{3,4},{4,5},{5,6},{6,7},{8,9},{9,10},{10,11},{11... | collective-permute-start | bytes 2359304 | tf_op jit(solution)/shard_map/ppermute | solution.py:300
  12.8 1.9 collective-permute-start.3
  14.8 3.3 %second.1 = (bf16[4,16,128,128]{3,2,1,0:T(8,128)(2,1)S(1)}, bf16[8,16,128,128]{3,2,1,0:T(8,128)(2,1)S(1)}, bf16[4,16,128,128]{3,2,1,0:T(8,128)(2,1)S(1)}, bf16[4...) custom-call(s32[8,16]{1,0:T(8,128)S(1)} %bitcast.23, bf16[4,16,128,128]{3,2,1,0:T(8,128)(2,1)S(1)} %get-tuple-element.33.raw_ref, ...), custom_call_target="tpu_custom_call" | custom-call | flops 536870912 | bytes 4194304 | tf_op jit(solution)/shard_map/second/pallas_call | solution.py:286
  18.1 3.6 %collective-permute-start = (bf16[4,6,128,128]{3,2,1,0:T(8,128)(2,1)S(1)}, bf16[4,6,128,128]{3,2,1,0:T(8,128)(2,1)S(1)}, u32[]{:S(2)}, u32[]{:S(2)}) collective-permute-start(bf16[4,6,128,128]{3,2,1,0:T(8,128)(2,1)S(1)} %get-tuple-element.38), channel_id=1, source_target_pairs={{0,1},{1,2},{2,3},{3,4},{4,5},{5,6},{6,7},{8,9},{9,10},{10,11},{11... | collective-permute-start | bytes 2359304 | tf_op jit(solution)/shard_map/ppermute | solution.py:300
  21.7 1.9 collective-permute-start.1
  23.7 2.5 %collective-permute-done.3.after_ref = bf16[4,6,128,128]{3,2,1,0:T(8,128)(2,1)S(1)} collective-permute-done((bf16[4,6,128,128]{3,2,1,0:T(8,128)(2,1)S(1)}, bf16[4,6,128,128]{3,2,1,0:T(8,128)(2,1)S(1)}, u32[]{:S(2)}, u32[]{:S(2)}) %collective-permute-start.3) | collective-permute-done | bytes 786464 | tf_op jit(solution)/shard_map/ppermute | solution.py:300
  26.1 6.7 %half.4.rest_0_ = bf16[16,8,128,128]{3,2,1,0:T(8,128)(2,1)S(1)} custom-call(f32[8,192]{1,0:T(8,128)S(1)} %reshape.44.w_ref, bf16[4,16,128,128]{3,2,1,0:T(8,128)(2,1)S(1)} %get-tuple-element.40.t_ref, bf16[4,16,128,128]{3,2,1,0:T(8,128)(2,1)S(1)} %get-tuple-element.41.c_ref, bf16[8,16,128,128]{3,2,1,0:T(8,128)(2,1)S(1)} %get-tuple-element.36.k_ref, ...), custom_call_target="tpu_custom_call" | custom-call | flops 1073741824 | bytes 4194304 | tf_op jit(solution)/shard_map/half/pallas_call | solution.py:322
  32.8 2.2 %collective-permute-done.1.after_ref = bf16[4,6,128,128]{3,2,1,0:T(8,128)(2,1)S(1)} collective-permute-done((bf16[4,6,128,128]{3,2,1,0:T(8,128)(2,1)S(1)}, bf16[4,6,128,128]{3,2,1,0:T(8,128)(2,1)S(1)}, u32[]{:S(2)}, u32[]{:S(2)}) %collective-permute-start.1) | collective-permute-done | bytes 786464 | tf_op jit(solution)/shard_map/ppermute | solution.py:300
  35.0 6.7 %half.5.h_ref = bf16[16,8,128,128]{3,2,1,0:T(8,128)(2,1)S(1)} custom-call(f32[8,192]{1,0:T(8,128)S(1)} %reshape.44.w_ref, bf16[4,16,128,128]{3,2,1,0:T(8,128)(2,1)S(1)} %get-tuple-element.35.t_ref, bf16[4,16,128,128]{3,2,1,0:T(8,128)(2,1)S(1)} %get-tuple-element.34.c_ref, ...), custom_call_target="tpu_custom_call", output_to_operand_aliasing={{}: (7, {})} | custom-call | flops 1073741824 | bytes 4194304 | tf_op jit(solution)/shard_map/half/pallas_call | solution.py:322
  41.8 62.8 %all_to_all.10 = bf16[128,1,128,128]{3,2,1,0:T(8,128)(2,1)S(1)} all-to-all(bf16[128,1,128,128]{3,2,1,0:T(8,128)(2,1)S(1)} %bitcast.17), channel_id=1, replica_groups=mesh['ia'=16,'ja'=8] {'ia','ja'}, dimensions={0} | all-to-all | bytes 8388608 | tf_op jit(solution)/shard_map/all_to_all | solution.py:368
  104.6 4.6 %middle.3 = (bf16[4,16,128,128]{3,2,1,0:T(8,128)(2,1)S(1)}, bf16[4,16,128,128]{3,2,1,0:T(8,128)(2,1)S(1)}, bf16[4,6,128,128]{3,2,1,0:T(8,128)(2,1)S(1)}, bf16[4,6,128,128]{3,2,1,0:T(8,128)(2,1)S(1)}) custom-call(s32[2]{0:T(128)S(1)} %pad_add_fusion.idx_ref, f32[128]{0:T(128)S(1)} %copy-done.3, s32[8,16]{1,0:T(8,128)S(1)} %bitcast.24, ...), custom_call_target="tpu_custom_call" | custom-call | flops 536870912 | bytes 2097152 | tf_op jit(solution)/shard_map/middle/pallas_call | solution.py:303
  109.2 2.9 %collective-permute-start.6 = (bf16[4,6,128,128]{3,2,1,0:T(8,128)(2,1)S(1)}, bf16[4,6,128,128]{3,2,1,0:T(8,128)(2,1)S(1)}, u32[]{:S(2)}, u32[]{:S(2)}) collective-permute-start(bf16[4,6,128,128]{3,2,1,0:T(8,128)(2,1)S(1)} %get-tuple-element.51), channel_id=1, source_target_pairs={{0,1},{1,2},{2,3},{3,4},{4,5},{5,6},{6,7},{8,9},{9,10},{10,11},{11... | collective-permute-start | bytes 2359304 | tf_op jit(solution)/shard_map/ppermute | solution.py:300
  112.1 1.9 collective-permute-start.7
  114.0 4.6 %middle.2 = (bf16[4,16,128,128]{3,2,1,0:T(8,128)(2,1)S(1)}, bf16[4,16,128,128]{3,2,1,0:T(8,128)(2,1)S(1)}, bf16[4,6,128,128]{3,2,1,0:T(8,128)(2,1)S(1)}, bf16[4,6,128,128]{3,2,1,0:T(8,128)(2,1)S(1)}) custom-call(s32[2]{0:T(128)S(1)} %pad_add_fusion.idx_ref, f32[128]{0:T(128)S(1)} %copy-done.3, s32[8,16]{1,0:T(8,128)S(1)} %bitcast.25, ...), custom_call_target="tpu_custom_call" | custom-call | flops 536870912 | bytes 2097152 | tf_op jit(solution)/shard_map/middle/pallas_call | solution.py:303
  118.6 3.6 %collective-permute-start.4 = (bf16[4,6,128,128]{3,2,1,0:T(8,128)(2,1)S(1)}, bf16[4,6,128,128]{3,2,1,0:T(8,128)(2,1)S(1)}, u32[]{:S(2)}, u32[]{:S(2)}) collective-permute-start(bf16[4,6,128,128]{3,2,1,0:T(8,128)(2,1)S(1)} %get-tuple-element.47), channel_id=1, source_target_pairs={{0,1},{1,2},{2,3},{3,4},{4,5},{5,6},{6,7},{8,9},{9,10},{10,11},{11... | collective-permute-start | bytes 2359304 | tf_op jit(solution)/shard_map/ppermute | solution.py:300
  122.3 1.9 collective-permute-start.5
  124.2 1.2 collective-permute-done.7.after_ref
  125.4 6.7 %half.6.rest_0_ = bf16[16,8,128,128]{3,2,1,0:T(8,128)(2,1)S(1)} custom-call(f32[8,192]{1,0:T(8,128)S(1)} %reshape.44.w_ref, bf16[4,16,128,128]{3,2,1,0:T(8,128)(2,1)S(1)} %get-tuple-element.49.t_ref.rest_0_, bf16[4,16,128,128]{3,2,1,0:T(8,128)(2,1)S(1)} %get-tuple-element.41.c_ref, bf16[8,16,128,128]{3,2,1,0:T(8,128)(2,1)S(1)} %get-tuple-element.36.k_ref, ...), custom_call_target="tpu_custom_call" | custom-call | flops 1073741824 | bytes 4194304 | tf_op jit(solution)/shard_map/half/pallas_call | solution.py:322
  132.1 3.5 %collective-permute-done.5.after_ref = bf16[4,6,128,128]{3,2,1,0:T(8,128)(2,1)S(1)} collective-permute-done((bf16[4,6,128,128]{3,2,1,0:T(8,128)(2,1)S(1)}, bf16[4,6,128,128]{3,2,1,0:T(8,128)(2,1)S(1)}, u32[]{:S(2)}, u32[]{:S(2)}) %collective-permute-start.5) | collective-permute-done | bytes 786464 | tf_op jit(solution)/shard_map/ppermute | solution.py:300
  135.6 6.8 %half.7.h_ref = bf16[16,8,128,128]{3,2,1,0:T(8,128)(2,1)S(1)} custom-call(f32[8,192]{1,0:T(8,128)S(1)} %reshape.44.w_ref, bf16[4,16,128,128]{3,2,1,0:T(8,128)(2,1)S(1)} %get-tuple-element.45.t_ref.rest_1_, bf16[4,16,128,128]{3,2,1,0:T(8,128)(2,1)S(1)} %get-tuple-element.34.c_ref, ...), custom_call_target="tpu_custom_call", output_to_operand_aliasing={{}: (7, {})} | custom-call | flops 1073741824 | bytes 4194304 | tf_op jit(solution)/shard_map/half/pallas_call | solution.py:322
  142.3 56.5 %all_to_all.11 = bf16[128,1,128,128]{3,2,1,0:T(8,128)(2,1)S(1)} all-to-all(bf16[128,1,128,128]{3,2,1,0:T(8,128)(2,1)S(1)} %bitcast.18), channel_id=1, replica_groups=mesh['ia'=16,'ja'=8] {'ia','ja'}, dimensions={0} | all-to-all | bytes 8388608 | tf_op jit(solution)/shard_map/all_to_all | solution.py:368
  198.8 7.1 %last.1 = bf16[8,1,16,128,128]{4,3,2,1,0:T(8,128)(2,1)} custom-call(s32[2]{0:T(128)S(1)} %pad_add_fusion.idx_ref, f32[128]{0:T(128)S(1)} %copy-done.3, s32[8,16]{1,0:T(8,128)S(1)} %bitcast.26, f32[8,1,16,128]{3,2,1,0:T(8,128)S(1)} %copy-done, bf16[16,8,128,128]{3,2,1,0:T(8,128)(2,1)S(1)} %half.7.h_ref, bf16[16,8,128,128]{3,2,1,0:T(8,128)(2,1)S(1)} %bitcast.21, ...), custom_call_target="tpu_custom_call" | custom-call | bytes 8388608 | tf_op jit(solution)/shard_map/last/pallas_call | solution.py:335
  (11 shorter events, 0.0 us)
Async XLA Ops:
  2.9 0.7 copy-start.1
  8.2 15.4 %collective-permute-start.2 = (bf16[4,6,128,128]{3,2,1,0:T(8,128)(2,1)S(1)}, bf16[4,6,128,128]{3,2,1,0:T(8,128)(2,1)S(1)}, u32[]{:S(2)}, u32[]{:S(2)}) collective-permute-start(bf16[4,6,128,128]{3,2,1,0:T(8,128)(2,1)S(1)} %get-tuple-element.43), channel_id=1, source_target_pairs={{0,1},{1,2},{2,3},{3,4},{4,5},{5,6},{6,7},{8,9},{9,10},{10,11},{11... | collective-permute-start | bytes 2359304 | tf_op jit(solution)/shard_map/ppermute | solution.py:300
  12.8 13.3 %collective-permute-start.3 = (bf16[4,6,128,128]{3,2,1,0:T(8,128)(2,1)S(1)}, bf16[4,6,128,128]{3,2,1,0:T(8,128)(2,1)S(1)}, u32[]{:S(2)}, u32[]{:S(2)}) collective-permute-start(bf16[4,6,128,128]{3,2,1,0:T(8,128)(2,1)S(1)} %get-tuple-element.44), channel_id=1, source_target_pairs={{1,0},{2,1},{3,2},{4,3},{5,4},{6,5},{7,6},{9,8},{10,9},{11,10},{12... | collective-permute-start | bytes 2359304 | tf_op jit(solution)/shard_map/ppermute | solution.py:300
  18.1 14.8 %collective-permute-start = (bf16[4,6,128,128]{3,2,1,0:T(8,128)(2,1)S(1)}, bf16[4,6,128,128]{3,2,1,0:T(8,128)(2,1)S(1)}, u32[]{:S(2)}, u32[]{:S(2)}) collective-permute-start(bf16[4,6,128,128]{3,2,1,0:T(8,128)(2,1)S(1)} %get-tuple-element.38), channel_id=1, source_target_pairs={{0,1},{1,2},{2,3},{3,4},{4,5},{5,6},{6,7},{8,9},{9,10},{10,11},{11... | collective-permute-start | bytes 2359304 | tf_op jit(solution)/shard_map/ppermute | solution.py:300
  21.7 13.3 %collective-permute-start.1 = (bf16[4,6,128,128]{3,2,1,0:T(8,128)(2,1)S(1)}, bf16[4,6,128,128]{3,2,1,0:T(8,128)(2,1)S(1)}, u32[]{:S(2)}, u32[]{:S(2)}) collective-permute-start(bf16[4,6,128,128]{3,2,1,0:T(8,128)(2,1)S(1)} %get-tuple-element.39), channel_id=1, source_target_pairs={{1,0},{2,1},{3,2},{4,3},{5,4},{6,5},{7,6},{9,8},{10,9},{11,10},{12... | collective-permute-start | bytes 2359304 | tf_op jit(solution)/shard_map/ppermute | solution.py:300
  41.8 62.8 %copy-start = (f32[8,1,16,128]{3,2,1,0:T(8,128)S(1)}, f32[8,1,16,128]{3,2,1,0:T(8,128)}, u32[]{:S(2)}) copy-start(f32[8,1,16,128]{3,2,1,0:T(8,128)} %e_ref.5) | copy-start | bytes 196612
  41.8 62.8 %copy-start.2 = (s32[8,1,16]{2,1,0:T(1,128)S(1)}, s32[8,1,16]{2,1,0:T(1,128)}, u32[]{:S(2)}) copy-start(s32[8,1,16]{2,1,0:T(1,128)} %param.13) | copy-start | bytes 1540
  41.8 62.8 %copy-start.3 = (f32[128]{0:T(128)S(1)}, f32[128]{0:T(128)}, u32[]{:S(2)}) copy-start(f32[128]{0:T(128)} %occ_ref.5) | copy-start | bytes 1540
  109.2 15.0 %collective-permute-start.6 = (bf16[4,6,128,128]{3,2,1,0:T(8,128)(2,1)S(1)}, bf16[4,6,128,128]{3,2,1,0:T(8,128)(2,1)S(1)}, u32[]{:S(2)}, u32[]{:S(2)}) collective-permute-start(bf16[4,6,128,128]{3,2,1,0:T(8,128)(2,1)S(1)} %get-tuple-element.51), channel_id=1, source_target_pairs={{0,1},{1,2},{2,3},{3,4},{4,5},{5,6},{6,7},{8,9},{9,10},{10,11},{11... | collective-permute-start | bytes 2359304 | tf_op jit(solution)/shard_map/ppermute | solution.py:300
  112.1 13.3 %collective-permute-start.7 = (bf16[4,6,128,128]{3,2,1,0:T(8,128)(2,1)S(1)}, bf16[4,6,128,128]{3,2,1,0:T(8,128)(2,1)S(1)}, u32[]{:S(2)}, u32[]{:S(2)}) collective-permute-start(bf16[4,6,128,128]{3,2,1,0:T(8,128)(2,1)S(1)} %get-tuple-element.52), channel_id=1, source_target_pairs={{1,0},{2,1},{3,2},{4,3},{5,4},{6,5},{7,6},{9,8},{10,9},{11,10},{12... | collective-permute-start | bytes 2359304 | tf_op jit(solution)/shard_map/ppermute | solution.py:300
  118.6 13.5 %collective-permute-start.4 = (bf16[4,6,128,128]{3,2,1,0:T(8,128)(2,1)S(1)}, bf16[4,6,128,128]{3,2,1,0:T(8,128)(2,1)S(1)}, u32[]{:S(2)}, u32[]{:S(2)}) collective-permute-start(bf16[4,6,128,128]{3,2,1,0:T(8,128)(2,1)S(1)} %get-tuple-element.47), channel_id=1, source_target_pairs={{0,1},{1,2},{2,3},{3,4},{4,5},{5,6},{6,7},{8,9},{9,10},{10,11},{11... | collective-permute-start | bytes 2359304 | tf_op jit(solution)/shard_map/ppermute | solution.py:300
  122.3 13.3 %collective-permute-start.5 = (bf16[4,6,128,128]{3,2,1,0:T(8,128)(2,1)S(1)}, bf16[4,6,128,128]{3,2,1,0:T(8,128)(2,1)S(1)}, u32[]{:S(2)}, u32[]{:S(2)}) collective-permute-start(bf16[4,6,128,128]{3,2,1,0:T(8,128)(2,1)S(1)} %get-tuple-element.48), channel_id=1, source_target_pairs={{1,0},{2,1},{3,2},{4,3},{5,4},{6,5},{7,6},{9,8},{10,9},{11,10},{12... | collective-permute-start | bytes 2359304 | tf_op jit(solution)/shard_map/ppermute | solution.py:300

commit v2 on v1

v2 whole, which is shorter than its diff:
```python
from functools import partial

import jax
import jax.numpy as jnp
from jax import lax
from jax.experimental import pallas as pl
from jax.experimental.pallas import tpu as pltpu
from jax.sharding import PartitionSpec as P

WIN = 6
ITERS = 2
DAMPING = 0.5
GROUPS = 2
SKEW = 4
VMEM_BYTES = 16 * 1024 * 1024

BF = jnp.bfloat16
F32 = jnp.float32


def window_shift(slot_index):
    return slot_index - WIN if slot_index < WIN else slot_index - WIN + 1


def nn(a, b):
    return lax.dot_general(a, b, (((1,), (0,)), ((), ())), preferred_element_type=F32)


def nt(a, b):
    return lax.dot_general(a, b, (((1,), (1,)), ((), ())), preferred_element_type=F32)


def tn(a, b):
    return lax.dot_general(a, b, (((0,), (0,)), ((), ())), preferred_element_type=F32)


def inside_mask(count, virtuals):
    rows = lax.broadcasted_iota(jnp.int32, (virtuals, virtuals), 0)
    cols = lax.broadcasted_iota(jnp.int32, (virtuals, virtuals), 1)
    return jnp.maximum(rows, cols) < count


def back_forms(f, parity, amps, coef, x_ref, near_ref, far_ref):
    columns = x_ref.shape[1]
    ready, leading = {}, {}
    for step in range(columns + 2 * SKEW):
        b = step
        if b < columns:
            ready[b] = amps(b)
        b = step - SKEW
        if 0 <= b < columns:
            leading[b] = nn(coef(b), ready.pop(b)).astype(BF)
        b = step - 2 * SKEW
        if 0 <= b:
            x_ref[f, b] = nt(leading.pop(b), coef(b)).astype(BF)
    edge = columns - WIN
    near_ref[f] = x_ref[f, pl.ds((1 - parity) * edge, WIN)]
    far_ref[f] = x_ref[f, pl.ds(parity * edge, WIN)]


def masked_forms(f, offset, parity, counts_ref, raw_ref, c_ref, tm_ref, x_ref, near_ref, far_ref):
    virtuals = x_ref.shape[2]

    def amps(b):
        keep = inside_mask(counts_ref[f + offset, 0, b], virtuals)
        value = jnp.where(keep, raw_ref[f, b].astype(F32), 0.0).astype(BF)
        tm_ref[f, b] = value
        return value

    back_forms(f, parity, amps, lambda b: c_ref[f, b], x_ref, near_ref, far_ref)


def start_kernel(
    counts_hbm, t_hbm, c_hbm, tm_ref, c_ref, raw_next, c_next, x_ref, near_ref, far_ref,
    raw_ref, counts_ref, sems, next_sems,
):
    size = x_ref.shape[0]
    parity = lax.rem(lax.axis_index("ja"), 2)

    def loads(f):
        return (
            pltpu.make_async_copy(t_hbm.at[f, 0], raw_ref.at[f], sems.at[f, 0]),
            pltpu.make_async_copy(c_hbm.at[f, 0], c_ref.at[f], sems.at[f, 1]),
        )

    for f in range(size):
        for load in loads(f):
            load.start()
    number = pltpu.make_async_copy(counts_hbm, counts_ref, next_sems.at[2])
    number.start()
    rest = pl.ds(size, size)
    later = (
        pltpu.make_async_copy(t_hbm.at[rest, 0], raw_next, next_sems.at[0]),
        pltpu.make_async_copy(c_hbm.at[rest, 0], c_next, next_sems.at[1]),
    )
    for load in later:
        load.start()
    number.wait()

    def body(f, carry):
        for load in loads(f):
            load.wait()
        masked_forms(f, 0, parity, counts_ref, raw_ref, c_ref, tm_ref, x_ref, near_ref, far_ref)
        return carry

    lax.fori_loop(0, size, body, 0)
    for load in later:
        load.wait()


def second_kernel(
    counts_ref, raw_ref, c_ref, k_hbm, tm_ref, k_ref, x_ref, near_ref, far_ref, sems
):
    size = x_ref.shape[0]
    parity = lax.rem(lax.axis_index("ja"), 2)
    load = pltpu.make_async_copy(k_hbm.at[:, 0], k_ref, sems.at[0])
    load.start()

    def body(f, carry):
        masked_forms(f, size, parity, counts_ref, raw_ref, c_ref, tm_ref, x_ref, near_ref, far_ref)
        return carry

    lax.fori_loop(0, size, body, 0)
    load.wait()


def updated(f, b, offset, occ_ref, counts_ref, rows_energy, e_ref, h_ref, p_ref, t_ref):
    columns, virtuals = t_ref.shape[1:3]
    occ_row = occ_ref[(f + offset) * columns + lax.axis_index("ia")]
    occ_col = occ_ref[lax.axis_index("ja") * columns + b]
    cols_energy = e_ref[f + offset, 0, b : b + 1, :]
    denominator = (rows_energy[:, b : b + 1] - occ_row) + (cols_energy - occ_col)
    inverse = pl.reciprocal(denominator)
    residual = h_ref[b, f + offset].astype(F32) + p_ref[b, f + offset].T.astype(F32)
    stepped = (1.0 - DAMPING) * t_ref[f, b].astype(F32) - (DAMPING * residual) * inverse
    keep = inside_mask(counts_ref[f + offset, 0, b], virtuals)
    return jnp.where(keep, stepped, 0.0).astype(BF)


def middle_kernel(
    offset, occ_ref, counts_ref, e_ref, h_ref, p_ref, t_ref, c_ref,
    tm_ref, x_ref, near_ref, far_ref,
):
    parity = lax.rem(lax.axis_index("ja"), 2)

    def body(f, carry):
        rows_energy = e_ref[f + offset, 0].T

        def amps(b):
            value = updated(
                f, b, offset, occ_ref, counts_ref, rows_energy, e_ref, h_ref, p_ref, t_ref
            )
            tm_ref[f, b] = value
            return value

        back_forms(f, parity, amps, lambda b: c_ref[f, b], x_ref, near_ref, far_ref)
        return carry

    lax.fori_loop(0, x_ref.shape[0], body, 0)


def last_kernel(occ_ref, counts_ref, e_ref, h_ref, p_ref, *rest):
    out_hbm, made_ref, sems = rest[-3:]
    t_refs = rest[:-3]
    size, columns = t_refs[0].shape[:2]

    def store(f):
        return pltpu.make_async_copy(made_ref.at[f], out_hbm.at[f, 0], sems.at[f])

    for g, t_ref in enumerate(t_refs):
        offset = g * size

        def body(f, carry, offset=offset, t_ref=t_ref):
            rows_energy = e_ref[f + offset, 0].T
            for b in range(columns):
                made_ref[f + offset, b] = updated(
                    f, b, offset, occ_ref, counts_ref, rows_energy, e_ref, h_ref, p_ref, t_ref
                )
            store(f + offset).start()
            return carry

        lax.fori_loop(0, size, body, 0)
    for f in range(len(t_refs) * size):
        store(f).wait()


def weights_kernel(coupled_ref, fock_ref, w_ref):
    orbitals = fock_ref.shape[0]
    slots, columns = 2 * WIN, coupled_ref.shape[2]
    rows = lax.broadcasted_iota(jnp.int32, (orbitals, orbitals), 0)
    cols = lax.broadcasted_iota(jnp.int32, (orbitals, orbitals), 1)
    turn = lax.rem(orbitals - lax.axis_index("ja") * columns, orbitals)
    for s in range(slots):
        band = jnp.where(rows == cols + window_shift(s), fock_ref[...], 0.0)
        band = pltpu.roll(jnp.sum(band, axis=0, keepdims=True), turn, 1)[:, :columns]
        for f in range(coupled_ref.shape[0] // slots):
            w_ref[f * slots + s] = -(coupled_ref[f * slots + s].astype(F32) * band)


def half_kernel(offset, w_ref, t_ref, c_ref, k_ref, x_ref, near_ref, far_ref, *rest):
    h_ref, xf = rest[-2:]
    size, columns, virtuals = x_ref.shape[:3]
    lag = columns // 2
    parity = lax.rem(lax.axis_index("ja"), 2)

    def body(f, carry):
        xf[pl.ds((1 - parity) * (WIN + columns), WIN)] = near_ref[f].astype(F32)
        xf[pl.ds(parity * (WIN + columns), WIN)] = far_ref[f].astype(F32)
        xf[WIN : WIN + columns] = x_ref[f].astype(F32)
        window, left_proj, left_quad = {}, {}, {}
        for step in range(columns + 2 * lag):
            b = step
            if b < columns:
                total = w_ref[(f + offset) * 2 * WIN, 0, b] * xf[b + WIN + window_shift(0)]
                for s in range(1, 2 * WIN):
                    total = total + w_ref[(f + offset) * 2 * WIN + s, 0, b] * xf[b + WIN + window_shift(s)]
                window[b] = total.astype(BF)
            b = step - lag
            if 0 <= b < columns:
                left_proj[b] = tn(c_ref[f, b], window.pop(b)).astype(BF)
                left_quad[b] = (nn(t_ref[f, b], k_ref[f + offset, b]) * (1.0 / virtuals)).astype(BF)
            b = step - 2 * lag
            if 0 <= b:
                joined = nn(
                    jnp.concatenate([left_quad.pop(b), left_proj.pop(b)], axis=1),
                    jnp.concatenate([t_ref[f, b], c_ref[f, b]], axis=0),
                )
                h_ref[b, f + offset] = (0.5 * k_ref[f + offset, b].astype(F32) + joined).astype(BF)
        return carry

    lax.fori_loop(0, size, body, 0)


SMEM = pl.BlockSpec(memory_space=pltpu.SMEM)
VMEM = pl.BlockSpec(memory_space=pltpu.VMEM)
HBM = pl.BlockSpec(memory_space=pltpu.HBM)


def params():
    return pltpu.CompilerParams(vmem_limit_bytes=VMEM_BYTES)


def near_core(value):
    return pltpu.with_memory_space_constraint(value, pltpu.VMEM)


def far(value):
    return pltpu.with_memory_space_constraint(value, pltpu.HBM)


def cost(flops, moved):
    return pl.CostEstimate(flops=flops, bytes_accessed=moved, transcendentals=0)


def on_device(
    amplitudes, coefficients, integrals, pno_energy, pno_counts, coupled, occ_fock, occ_energy
):
    fragments, _, columns, virtuals, _ = amplitudes.shape
    size = fragments // GROUPS
    pairs = size * columns
    matmul = 2 * virtuals**3 * pairs
    block = 2 * virtuals**2 * pairs
    listed = jnp.transpose(coupled, (0, 3, 1, 2)).reshape(fragments * 2 * WIN, 1, columns)
    counts = pno_counts
    energies = near_core(pno_energy)

    peers = lax.axis_size("ja")
    near_pairs = [(i, i ^ 1) for i in range(peers)]
    far_pairs = [(i, i + 1 if i % 2 else i - 1) for i in range(1, peers - 1)]

    def near_shape(*lead):
        return pltpu.VMEM((*lead, virtuals, virtuals), BF)

    group = near_shape(size, columns)
    back = [group, near_shape(size, WIN), near_shape(size, WIN)]

    def first_steps():
        tm, c, raw_next, c_next, *made = pl.pallas_call(
            start_kernel,
            in_specs=[HBM, HBM, HBM],
            out_shape=[group] * 4 + back,
            out_specs=[VMEM] * 7,
            scratch_shapes=[
                pltpu.VMEM((size, columns, virtuals, virtuals), BF),
                pltpu.SMEM(counts.shape, jnp.int32),
                pltpu.SemaphoreType.DMA((size, 2)),
                pltpu.SemaphoreType.DMA((3,)),
            ],
            compiler_params=params(),
            cost_estimate=cost(2 * matmul, 4 * block),
            name="start",
        )(far(counts), far(amplitudes), far(coefficients))
        borders = [exchange(made)]
        tm_next, k, *made_next = pl.pallas_call(
            second_kernel,
            in_specs=[SMEM, VMEM, VMEM, HBM],
            out_shape=[group, near_shape(fragments, columns)] + back,
            out_specs=[VMEM] * 5,
            scratch_shapes=[pltpu.SemaphoreType.DMA((1,))],
            compiler_params=params(),
            cost_estimate=cost(2 * matmul, 2 * block),
            name="second",
        )(counts, near_core(raw_next), near_core(c_next), far(integrals))
        borders.append(exchange(made_next))
        weights = pl.pallas_call(
            weights_kernel,
            in_specs=[VMEM, VMEM],
            out_shape=jax.ShapeDtypeStruct(listed.shape, F32),
            out_specs=VMEM,
            compiler_params=params(),
            cost_estimate=cost(0, block // 8),
            name="weights",
        )(*lax.optimization_barrier((listed, occ_fock, tm_next))[:2])
        return [tm, tm_next], [c, c_next], k, [made[0], made_next[0]], borders, weights

    def exchange(made):
        return lax.ppermute(made[1], "ja", near_pairs), lax.ppermute(made[2], "ja", far_pairs)

    def next_step(g, halves, partner, current, coefs):
        return pl.pallas_call(
            partial(middle_kernel, g * size),
            in_specs=[SMEM] * 2 + [VMEM] * 5,
            out_shape=[group] + back,
            out_specs=[VMEM] * 4,
            compiler_params=params(),
            cost_estimate=cost(2 * matmul, block),
            name="middle",
        )(
            occ_energy, counts, energies, near_core(halves), near_core(partner),
            near_core(current[g]), near_core(coefs[g]),
        )

    def half_step(g, weights, current, coefs, ints, back_form, from_near, from_far, out):
        operands = [current[g], coefs[g], ints, back_form, from_near, from_far]
        aliases = {}
        if out is not None:
            aliases = {len(operands) + 1: 0}
            operands.append(out)
        return pl.pallas_call(
            partial(half_kernel, g * size),
            in_specs=[SMEM] + [VMEM] * len(operands),
            out_shape=near_shape(columns, fragments),
            out_specs=VMEM,
            scratch_shapes=[pltpu.VMEM((columns + 2 * WIN, virtuals, virtuals), F32)],
            input_output_aliases=aliases,
            compiler_params=params(),
            cost_estimate=cost(4 * matmul, 2 * block),
            name="half",
        )(weights, *map(near_core, operands))

    def last_step(halves, partner, current):
        return pl.pallas_call(
            last_kernel,
            in_specs=[SMEM] * 2 + [VMEM] * (3 + GROUPS),
            out_shape=pltpu.HBM(amplitudes.shape, BF),
            out_specs=HBM,
            scratch_shapes=[
                pltpu.VMEM((fragments, columns, virtuals, virtuals), BF),
                pltpu.SemaphoreType.DMA((fragments,)),
            ],
            compiler_params=params(),
            cost_estimate=cost(0, 2 * GROUPS * block),
            name="last",
        )(
            occ_energy, counts, energies, near_core(halves), near_core(partner),
            *map(near_core, current),
        )

    halves = partner = None
    for sweep in range(ITERS):
        if sweep == 0:
            current, coefs, ints, back_form, borders, weights = first_steps()
        else:
            new, back_form, borders = [], [], []
            for g in range(GROUPS):
                tm, *made = next_step(g, halves, partner, current, coefs)
                borders.append(exchange(made))
                new.append(tm)
                back_form.append(made[0])
            current = new
        halves = None
        for g in range(GROUPS):
            halves = half_step(g, weights, current, coefs, ints, back_form[g], *borders[g], halves)
        sent = halves.reshape(columns * fragments, 1, virtuals, virtuals)
        arrived = lax.all_to_all(sent, ("ia", "ja"), split_axis=0, concat_axis=0, tiled=True)
        partner = arrived.reshape(columns, fragments, virtuals, virtuals)
    return last_step(halves, partner, current)


def solution(mesh):
    placed = (
        P(None, "ia", "ja", None, None),
        P(None, "ia", "ja", None, None),
        P(None, "ia", "ja", None, None),
        P(None, "ia", "ja", None),
        P(None, "ia", "ja"),
        P(None, "ia", "ja", None),
        P(),
        P(),
    )
    return jax.shard_map(
        on_device,
        mesh=mesh,
        in_specs=placed,
        out_specs=P(None, "ia", "ja", None, None),
        check_vma=False,
    )
```

time: 206 us -> 196 us (0.951)
  starting transfers between devices: 22.4 us -> 14.9 us
  Pallas kernels: 51.1 us -> 54.1 us
    ppermute x8, starting transfers between devices: 22.4 us -> 14.9 us  [the longest x4 12.3 us: exchange(): lax.ppermute(made[2], 'ja', far_pairs)]
    pallas_call x4, Pallas kernels: 26.9 us -> 30 us  [half_step(): pl.pallas_call(partial(half_kernel, g * size), in_specs=[SMEM] + [VMEM] *...]
    pallas_call x4 -> x5, Pallas kernels: 20.9 us -> 20.7 us  [the longest x2 9.38 us: next_step(): pl.pallas_call(partial(middle_kernel, g * size), in_specs=[SMEM] * 2 + [V...]
  transfers between devices with their start and end apart: 8 -> 8, of which waited for: 4 -> 4; matrix products, arithmetic and copies ran while one was open for 0% -> 0% of each run, Pallas kernels for 10% -> 12%
where the time goes in v2:
time: 196 us
  blocking collectives  119 us (61%)
  Pallas kernels  54.1 us (28%)
  starting transfers between devices  14.9 us (8%)
  waiting for transfers between devices  7.58 us (4%)
    all_to_all x2, blocking collectives, on_device(): lax.all_to_all(sent, ('ia', 'ja'), split_axis=0, concat_axis=0, tiled=True)  119 us
    pallas_call x4, Pallas kernels, half_step(): pl.pallas_call(partial(half_kernel, g * size), in_specs=[SMEM] + [VMEM] *...  30 us
    ppermute x4, starting transfers between devices, exchange(): lax.ppermute(made[2], 'ja', far_pairs)  12.3 us
    pallas_call x2, Pallas kernels, next_step(): pl.pallas_call(partial(middle_kernel, g * size), in_specs=[SMEM] * 2 + [V...  9.38 us
    ppermute x4, waiting for transfers between devices, exchange(): lax.ppermute(made[2], 'ja', far_pairs)  7.57 us
    pallas_call x1, Pallas kernels, last_step(): pl.pallas_call(last_kernel, in_specs=[SMEM] * 2 + [VMEM] * (3 + GROUPS),...  7.02 us
    pallas_call x1, Pallas kernels, first_steps(): pl.pallas_call(start_kernel, in_specs=[HBM, HBM, HBM], out_shape=[group]...  4.1 us
  transfers between devices with their start and end apart: 8, of which 4 were waited for; matrix products, arithmetic and copies ran while one was open for 0% of the time, Pallas kernels for 12%

profile of v2, /device:TPU:1, one launch (start us, length us, event | category | flops | bytes accessed | tf_op | source)
XLA Modules:
  0.0 196.1 jit_solution(4370680214133993743)
XLA Ops:
  0.0 4.1 %start.1 = (bf16[4,16,128,128]{3,2,1,0:T(8,128)(2,1)S(1)}, bf16[4,16,128,128]{3,2,1,0:T(8,128)(2,1)S(1)}, bf16[4,16,128,128]{3,2,1,0:T(8,128)(2,1)S(1)}, bf16[4,...) custom-call(s32[8,1,16]{2,1,0:T(1,128)} %counts_ref.7, ...), custom_call_target="tpu_custom_call" | custom-call | flops 536870912 | bytes 8388608 | tf_op jit(solution)/shard_map/start/pallas_call | solution.py:278
  4.1 1.5 collective-permute-start.2
  5.6 3.2 %collective-permute-start.3 = (bf16[4,6,128,128]{3,2,1,0:T(8,128)(2,1)S(1)}, bf16[4,6,128,128]{3,2,1,0:T(8,128)(2,1)S(1)}, u32[]{:S(2)}, u32[]{:S(2)}) collective-permute-start(bf16[4,6,128,128]{3,2,1,0:T(8,128)(2,1)S(1)} %get-tuple-element.40), channel_id=1, source_target_pairs={{1,2},{2,1},{3,4},{4,3},{5,6},{6,5},{9,10},{10,9},{11,12},{12,11},... | collective-permute-start | bytes 2359304 | tf_op jit(solution)/shard_map/ppermute | solution.py:317
  8.8 0.0 copy-start.2
  8.8 0.0 copy-start.3
  8.8 3.4 %second.1 = (bf16[4,16,128,128]{3,2,1,0:T(8,128)(2,1)S(1)}, bf16[8,16,128,128]{3,2,1,0:T(8,128)(2,1)S(1)}, bf16[4,16,128,128]{3,2,1,0:T(8,128)(2,1)S(1)}, bf16[4...) custom-call(s32[8,1,16]{2,1,0:T(1,128)S(1)} %copy-done.1, ...), custom_call_target="tpu_custom_call" | custom-call | flops 536870912 | bytes 4194304 | tf_op jit(solution)/shard_map/second/pallas_call | solution.py:294
  12.3 0.1 collective-permute-start
  12.4 3.6 %collective-permute-start.1 = (bf16[4,6,128,128]{3,2,1,0:T(8,128)(2,1)S(1)}, bf16[4,6,128,128]{3,2,1,0:T(8,128)(2,1)S(1)}, u32[]{:S(2)}, u32[]{:S(2)}) collective-permute-start(bf16[4,6,128,128]{3,2,1,0:T(8,128)(2,1)S(1)} %get-tuple-element.35), channel_id=1, source_target_pairs={{1,2},{2,1},{3,4},{4,3},{5,6},{6,5},{9,10},{10,9},{11,12},{12,11},... | collective-permute-start | bytes 2359304 | tf_op jit(solution)/shard_map/ppermute | solution.py:317
  16.0 0.2 weights.1.w_ref
  16.1 0.0 collective-permute-done.2.near_ref
  16.1 2.8 %collective-permute-done.3.far_ref = bf16[4,6,128,128]{3,2,1,0:T(8,128)(2,1)S(1)} collective-permute-done((bf16[4,6,128,128]{3,2,1,0:T(8,128)(2,1)S(1)}, bf16[4,6,128,128]{3,2,1,0:T(8,128)(2,1)S(1)}, u32[]{:S(2)}, u32[]{:S(2)}) %collective-permute-start.3) | collective-permute-done | bytes 786464 | tf_op jit(solution)/shard_map/ppermute | solution.py:317
  18.9 7.5 %half.4.rest_0_ = bf16[16,8,128,128]{3,2,1,0:T(8,128)(2,1)S(1)} custom-call(f32[96,1,16]{2,1,0:T(1,128)S(1)} %weights.1.w_ref, bf16[4,16,128,128]{3,2,1,0:T(8,128)(2,1)S(1)} %get-tuple-element.36.t_ref, bf16[4,16,128,128]{3,2,1,0:T(8,128)(2,1)S(1)} %get-tuple-element.37.c_ref, bf16[8,16,128,128]{3,2,1,0:T(8,128)(2,1)S(1)} %get-tuple-element.32.k_ref, ...), custom_call_target="tpu_custom_call" | custom-call | flops 1073741824 | bytes 4194304 | tf_op jit(solution)/shard_map/half/pallas_call | solution.py:339
  26.4 0.0 collective-permute-done.near_ref
  26.4 0.9 collective-permute-done.1.far_ref
  27.3 7.5 %half.5.h_ref = bf16[16,8,128,128]{3,2,1,0:T(8,128)(2,1)S(1)} custom-call(f32[96,1,16]{2,1,0:T(1,128)S(1)} %weights.1.w_ref, bf16[4,16,128,128]{3,2,1,0:T(8,128)(2,1)S(1)} %get-tuple-element.29.t_ref, bf16[4,16,128,128]{3,2,1,0:T(8,128)(2,1)S(1)} %get-tuple-element.28.c_ref, ...), custom_call_target="tpu_custom_call", output_to_operand_aliasing={{}: (7, {})} | custom-call | flops 1073741824 | bytes 4194304 | tf_op jit(solution)/shard_map/half/pallas_call | solution.py:339
  34.9 0.0 copy-start
  34.9 0.0 copy-start.4
  34.9 63.2 %all_to_all.10 = bf16[128,1,128,128]{3,2,1,0:T(8,128)(2,1)S(1)} all-to-all(bf16[128,1,128,128]{3,2,1,0:T(8,128)(2,1)S(1)} %bitcast.11), channel_id=1, replica_groups=mesh['ia'=16,'ja'=8] {'ia','ja'}, dimensions={0} | all-to-all | bytes 8388608 | tf_op jit(solution)/shard_map/all_to_all | solution.py:385
  98.1 4.7 %middle.3 = (bf16[4,16,128,128]{3,2,1,0:T(8,128)(2,1)S(1)}, bf16[4,16,128,128]{3,2,1,0:T(8,128)(2,1)S(1)}, bf16[4,6,128,128]{3,2,1,0:T(8,128)(2,1)S(1)}, bf16[4,6,128,128]{3,2,1,0:T(8,128)(2,1)S(1)}) custom-call(f32[128]{0:T(128)S(1)} %copy-done.4, s32[8,1,16]{2,1,0:T(1,128)S(1)} %copy-done.1, f32[8,1,16,128]{3,2,1,0:T(8,128)S(1)} %copy-done, ...), custom_call_target="tpu_custom_call" | custom-call | flops 536870912 | bytes 2097152 | tf_op jit(solution)/shard_map/middle/pallas_call | solution.py:320
  102.8 0.9 collective-permute-start.6
  103.7 2.0 %collective-permute-start.7 = (bf16[4,6,128,128]{3,2,1,0:T(8,128)(2,1)S(1)}, bf16[4,6,128,128]{3,2,1,0:T(8,128)(2,1)S(1)}, u32[]{:S(2)}, u32[]{:S(2)}) collective-permute-start(bf16[4,6,128,128]{3,2,1,0:T(8,128)(2,1)S(1)} %get-tuple-element.48), channel_id=1, source_target_pairs={{1,2},{2,1},{3,4},{4,3},{5,6},{6,5},{9,10},{10,9},{11,12},{12,11},... | collective-permute-start | bytes 2359304 | tf_op jit(solution)/shard_map/ppermute | solution.py:317
  105.7 4.7 %middle.2 = (bf16[4,16,128,128]{3,2,1,0:T(8,128)(2,1)S(1)}, bf16[4,16,128,128]{3,2,1,0:T(8,128)(2,1)S(1)}, bf16[4,6,128,128]{3,2,1,0:T(8,128)(2,1)S(1)}, bf16[4,6,128,128]{3,2,1,0:T(8,128)(2,1)S(1)}) custom-call(f32[128]{0:T(128)S(1)} %copy-done.4, s32[8,1,16]{2,1,0:T(1,128)S(1)} %copy-done.1, f32[8,1,16,128]{3,2,1,0:T(8,128)S(1)} %copy-done, ...), custom_call_target="tpu_custom_call" | custom-call | flops 536870912 | bytes 2097152 | tf_op jit(solution)/shard_map/middle/pallas_call | solution.py:320
  110.4 0.1 collective-permute-start.4
  110.5 3.5 %collective-permute-start.5 = (bf16[4,6,128,128]{3,2,1,0:T(8,128)(2,1)S(1)}, bf16[4,6,128,128]{3,2,1,0:T(8,128)(2,1)S(1)}, u32[]{:S(2)}, u32[]{:S(2)}) collective-permute-start(bf16[4,6,128,128]{3,2,1,0:T(8,128)(2,1)S(1)} %get-tuple-element.44), channel_id=1, source_target_pairs={{1,2},{2,1},{3,4},{4,3},{5,6},{6,5},{9,10},{10,9},{11,12},{12,11},... | collective-permute-start | bytes 2359304 | tf_op jit(solution)/shard_map/ppermute | solution.py:317
  114.0 0.0 collective-permute-done.6.near_ref
  114.1 2.9 %collective-permute-done.7.far_ref = bf16[4,6,128,128]{3,2,1,0:T(8,128)(2,1)S(1)} collective-permute-done((bf16[4,6,128,128]{3,2,1,0:T(8,128)(2,1)S(1)}, bf16[4,6,128,128]{3,2,1,0:T(8,128)(2,1)S(1)}, u32[]{:S(2)}, u32[]{:S(2)}) %collective-permute-start.7) | collective-permute-done | bytes 786464 | tf_op jit(solution)/shard_map/ppermute | solution.py:317
  117.0 7.5 %half.6.rest_0_ = bf16[16,8,128,128]{3,2,1,0:T(8,128)(2,1)S(1)} custom-call(f32[96,1,16]{2,1,0:T(1,128)S(1)} %weights.1.w_ref, bf16[4,16,128,128]{3,2,1,0:T(8,128)(2,1)S(1)} %get-tuple-element.45.t_ref.rest_0_, bf16[4,16,128,128]{3,2,1,0:T(8,128)(2,1)S(1)} %get-tuple-element.37.c_ref, bf16[8,16,128,128]{3,2,1,0:T(8,128)(2,1)S(1)} %get-tuple-element.32.k_ref, ...), custom_call_target="tpu_custom_call" | custom-call | flops 1073741824 | bytes 4194304 | tf_op jit(solution)/shard_map/half/pallas_call | solution.py:339
  124.5 0.0 collective-permute-done.4.near_ref
  124.5 0.9 collective-permute-done.5.far_ref
  125.4 7.5 %half.7.h_ref = bf16[16,8,128,128]{3,2,1,0:T(8,128)(2,1)S(1)} custom-call(f32[96,1,16]{2,1,0:T(1,128)S(1)} %weights.1.w_ref, bf16[4,16,128,128]{3,2,1,0:T(8,128)(2,1)S(1)} %get-tuple-element.41.t_ref.rest_1_, bf16[4,16,128,128]{3,2,1,0:T(8,128)(2,1)S(1)} %get-tuple-element.28.c_ref, ...), custom_call_target="tpu_custom_call", output_to_operand_aliasing={{}: (7, {})} | custom-call | flops 1073741824 | bytes 4194304 | tf_op jit(solution)/shard_map/half/pallas_call | solution.py:339
  133.0 56.1 %all_to_all.11 = bf16[128,1,128,128]{3,2,1,0:T(8,128)(2,1)S(1)} all-to-all(bf16[128,1,128,128]{3,2,1,0:T(8,128)(2,1)S(1)} %bitcast.12), channel_id=1, replica_groups=mesh['ia'=16,'ja'=8] {'ia','ja'}, dimensions={0} | all-to-all | bytes 8388608 | tf_op jit(solution)/shard_map/all_to_all | solution.py:385
  189.0 7.0 %last.1 = bf16[8,1,16,128,128]{4,3,2,1,0:T(8,128)(2,1)} custom-call(f32[128]{0:T(128)S(1)} %copy-done.4, s32[8,1,16]{2,1,0:T(1,128)S(1)} %copy-done.1, f32[8,1,16,128]{3,2,1,0:T(8,128)S(1)} %copy-done, bf16[16,8,128,128]{3,2,1,0:T(8,128)(2,1)S(1)} %half.7.h_ref, bf16[16,8,128,128]{3,2,1,0:T(8,128)(2,1)S(1)} %bitcast.15, ...), custom_call_target="tpu_custom_call" | custom-call | bytes 8388608 | tf_op jit(solution)/shard_map/last/pallas_call | solution.py:352
  (6 shorter events, 0.0 us)
Async XLA Ops:
  0.0 8.8 %copy-start.1 = (s32[8,1,16]{2,1,0:T(1,128)S(1)}, s32[8,1,16]{2,1,0:T(1,128)}, u32[]{:S(2)}) copy-start(s32[8,1,16]{2,1,0:T(1,128)} %counts_ref.7) | copy-start | bytes 1540
  4.1 12.0 %collective-permute-start.2 = (bf16[4,6,128,128]{3,2,1,0:T(8,128)(2,1)S(1)}, bf16[4,6,128,128]{3,2,1,0:T(8,128)(2,1)S(1)}, u32[]{:S(2)}, u32[]{:S(2)}) collective-permute-start(bf16[4,6,128,128]{3,2,1,0:T(8,128)(2,1)S(1)} %get-tuple-element.39), channel_id=1, source_target_pairs={{0,1},{1,0},{2,3},{3,2},{4,5},{5,4},{6,7},{7,6},{8,9},{9,8},{10,11... | collective-permute-start | bytes 2359304 | tf_op jit(solution)/shard_map/ppermute | solution.py:317
  5.6 13.3 %collective-permute-start.3 = (bf16[4,6,128,128]{3,2,1,0:T(8,128)(2,1)S(1)}, bf16[4,6,128,128]{3,2,1,0:T(8,128)(2,1)S(1)}, u32[]{:S(2)}, u32[]{:S(2)}) collective-permute-start(bf16[4,6,128,128]{3,2,1,0:T(8,128)(2,1)S(1)} %get-tuple-element.40), channel_id=1, source_target_pairs={{1,2},{2,1},{3,4},{4,3},{5,6},{6,5},{9,10},{10,9},{11,12},{12,11},... | collective-permute-start | bytes 2359304 | tf_op jit(solution)/shard_map/ppermute | solution.py:317
  8.8 7.1 %copy-start.2 = (f32[128,128]{1,0:T(8,128)S(1)}, f32[128,128]{1,0:T(8,128)}, u32[]{:S(2)}) copy-start(f32[128,128]{1,0:T(8,128)} %fock_ref) | copy-start | bytes 196612
  8.8 7.1 %copy-start.3 = (s32[8,1,16,12]{2,1,3,0:T(1,128)S(1)}, s32[8,1,16,12]{2,1,3,0:T(1,128)}, u32[]{:S(2)}) copy-start(s32[8,1,16,12]{2,1,3,0:T(1,128)} %param.13) | copy-start | bytes 18436
  12.3 14.1 %collective-permute-start = (bf16[4,6,128,128]{3,2,1,0:T(8,128)(2,1)S(1)}, bf16[4,6,128,128]{3,2,1,0:T(8,128)(2,1)S(1)}, u32[]{:S(2)}, u32[]{:S(2)}) collective-permute-start(bf16[4,6,128,128]{3,2,1,0:T(8,128)(2,1)S(1)} %get-tuple-element.34), channel_id=1, source_target_pairs={{0,1},{1,0},{2,3},{3,2},{4,5},{5,4},{6,7},{7,6},{8,9},{9,8},{10,11... | collective-permute-start | bytes 2359304 | tf_op jit(solution)/shard_map/ppermute | solution.py:317
  12.4 15.0 %collective-permute-start.1 = (bf16[4,6,128,128]{3,2,1,0:T(8,128)(2,1)S(1)}, bf16[4,6,128,128]{3,2,1,0:T(8,128)(2,1)S(1)}, u32[]{:S(2)}, u32[]{:S(2)}) collective-permute-start(bf16[4,6,128,128]{3,2,1,0:T(8,128)(2,1)S(1)} %get-tuple-element.35), channel_id=1, source_target_pairs={{1,2},{2,1},{3,4},{4,3},{5,6},{6,5},{9,10},{10,9},{11,12},{12,11},... | collective-permute-start | bytes 2359304 | tf_op jit(solution)/shard_map/ppermute | solution.py:317
  34.9 63.2 %copy-start = (f32[8,1,16,128]{3,2,1,0:T(8,128)S(1)}, f32[8,1,16,128]{3,2,1,0:T(8,128)}, u32[]{:S(2)}) copy-start(f32[8,1,16,128]{3,2,1,0:T(8,128)} %e_ref.5) | copy-start | bytes 196612
  34.9 63.2 %copy-start.4 = (f32[128]{0:T(128)S(1)}, f32[128]{0:T(128)}, u32[]{:S(2)}) copy-start(f32[128]{0:T(128)} %occ_ref.5) | copy-start | bytes 1540
  102.8 11.3 %collective-permute-start.6 = (bf16[4,6,128,128]{3,2,1,0:T(8,128)(2,1)S(1)}, bf16[4,6,128,128]{3,2,1,0:T(8,128)(2,1)S(1)}, u32[]{:S(2)}, u32[]{:S(2)}) collective-permute-start(bf16[4,6,128,128]{3,2,1,0:T(8,128)(2,1)S(1)} %get-tuple-element.47), channel_id=1, source_target_pairs={{0,1},{1,0},{2,3},{3,2},{4,5},{5,4},{6,7},{7,6},{8,9},{9,8},{10,11... | collective-permute-start | bytes 2359304 | tf_op jit(solution)/shard_map/ppermute | solution.py:317
  103.7 13.3 %collective-permute-start.7 = (bf16[4,6,128,128]{3,2,1,0:T(8,128)(2,1)S(1)}, bf16[4,6,128,128]{3,2,1,0:T(8,128)(2,1)S(1)}, u32[]{:S(2)}, u32[]{:S(2)}) collective-permute-start(bf16[4,6,128,128]{3,2,1,0:T(8,128)(2,1)S(1)} %get-tuple-element.48), channel_id=1, source_target_pairs={{1,2},{2,1},{3,4},{4,3},{5,6},{6,5},{9,10},{10,9},{11,12},{12,11},... | collective-permute-start | bytes 2359304 | tf_op jit(solution)/shard_map/ppermute | solution.py:317
  110.4 14.0 %collective-permute-start.4 = (bf16[4,6,128,128]{3,2,1,0:T(8,128)(2,1)S(1)}, bf16[4,6,128,128]{3,2,1,0:T(8,128)(2,1)S(1)}, u32[]{:S(2)}, u32[]{:S(2)}) collective-permute-start(bf16[4,6,128,128]{3,2,1,0:T(8,128)(2,1)S(1)} %get-tuple-element.43), channel_id=1, source_target_pairs={{0,1},{1,0},{2,3},{3,2},{4,5},{5,4},{6,7},{7,6},{8,9},{9,8},{10,11... | collective-permute-start | bytes 2359304 | tf_op jit(solution)/shard_map/ppermute | solution.py:317
  110.5 14.9 %collective-permute-start.5 = (bf16[4,6,128,128]{3,2,1,0:T(8,128)(2,1)S(1)}, bf16[4,6,128,128]{3,2,1,0:T(8,128)(2,1)S(1)}, u32[]{:S(2)}, u32[]{:S(2)}) collective-permute-start(bf16[4,6,128,128]{3,2,1,0:T(8,128)(2,1)S(1)} %get-tuple-element.44), channel_id=1, source_target_pairs={{1,2},{2,1},{3,4},{4,3},{5,6},{6,5},{9,10},{10,9},{11,12},{12,11},... | collective-permute-start | bytes 2359304 | tf_op jit(solution)/shard_map/ppermute | solution.py:317

commit v3 on v2

--- a/solution.py
+++ b/solution.py
@@ -10,7 +10,7 @@
 WIN = 6
 ITERS = 2
 DAMPING = 0.5
-GROUPS = 2
+GROUPS = ((4, 4), (4, 2, 2))
 SKEW = 4
 VMEM_BYTES = 16 * 1024 * 1024
 
@@ -124,80 +124,85 @@
     load.wait()
 
 
-def updated(f, b, offset, occ_ref, counts_ref, rows_energy, e_ref, h_ref, p_ref, t_ref):
-    columns, virtuals = t_ref.shape[1:3]
-    occ_row = occ_ref[(f + offset) * columns + lax.axis_index("ia")]
-    occ_col = occ_ref[lax.axis_index("ja") * columns + b]
-    cols_energy = e_ref[f + offset, 0, b : b + 1, :]
-    denominator = (rows_energy[:, b : b + 1] - occ_row) + (cols_energy - occ_col)
-    inverse = pl.reciprocal(denominator)
-    residual = h_ref[b, f + offset].astype(F32) + p_ref[b, f + offset].T.astype(F32)
-    stepped = (1.0 - DAMPING) * t_ref[f, b].astype(F32) - (DAMPING * residual) * inverse
-    keep = inside_mask(counts_ref[f + offset, 0, b], virtuals)
-    return jnp.where(keep, stepped, 0.0).astype(BF)
-
-
-def middle_kernel(
-    offset, occ_ref, counts_ref, e_ref, h_ref, p_ref, t_ref, c_ref,
-    tm_ref, x_ref, near_ref, far_ref,
-):
-    parity = lax.rem(lax.axis_index("ja"), 2)
-
-    def body(f, carry):
-        rows_energy = e_ref[f + offset, 0].T
-
-        def amps(b):
-            value = updated(
-                f, b, offset, occ_ref, counts_ref, rows_energy, e_ref, h_ref, p_ref, t_ref
-            )
-            tm_ref[f, b] = value
-            return value
-
-        back_forms(f, parity, amps, lambda b: c_ref[f, b], x_ref, near_ref, far_ref)
-        return carry
-
-    lax.fori_loop(0, x_ref.shape[0], body, 0)
-
-
-def last_kernel(occ_ref, counts_ref, e_ref, h_ref, p_ref, *rest):
-    out_hbm, made_ref, sems = rest[-3:]
-    t_refs = rest[:-3]
-    size, columns = t_refs[0].shape[:2]
-
-    def store(f):
-        return pltpu.make_async_copy(made_ref.at[f], out_hbm.at[f, 0], sems.at[f])
-
-    for g, t_ref in enumerate(t_refs):
-        offset = g * size
-
-        def body(f, carry, offset=offset, t_ref=t_ref):
-            rows_energy = e_ref[f + offset, 0].T
-            for b in range(columns):
-                made_ref[f + offset, b] = updated(
-                    f, b, offset, occ_ref, counts_ref, rows_energy, e_ref, h_ref, p_ref, t_ref
-                )
-            store(f + offset).start()
-            return carry
-
-        lax.fori_loop(0, size, body, 0)
-    for f in range(len(t_refs) * size):
-        store(f).wait()
-
-
-def weights_kernel(coupled_ref, fock_ref, w_ref):
+def gain_kernel(occ_ref, counts_ref, e_ref, coupled_ref, fock_ref, gain_ref, w_ref):
     orbitals = fock_ref.shape[0]
-    slots, columns = 2 * WIN, coupled_ref.shape[2]
+    fragments, columns, virtuals = gain_ref.shape[:3]
+    slots = 2 * WIN
     rows = lax.broadcasted_iota(jnp.int32, (orbitals, orbitals), 0)
     cols = lax.broadcasted_iota(jnp.int32, (orbitals, orbitals), 1)
     turn = lax.rem(orbitals - lax.axis_index("ja") * columns, orbitals)
     for s in range(slots):
         band = jnp.where(rows == cols + window_shift(s), fock_ref[...], 0.0)
         band = pltpu.roll(jnp.sum(band, axis=0, keepdims=True), turn, 1)[:, :columns]
-        for f in range(coupled_ref.shape[0] // slots):
-            w_ref[f * slots + s] = -(coupled_ref[f * slots + s].astype(F32) * band)
-
-
-def half_kernel(offset, w_ref, t_ref, c_ref, k_ref, x_ref, near_ref, far_ref, *rest):
+        parts = [coupled_ref[f * slots + s].astype(F32) * band for f in range(fragments)]
+        w_ref[s : s + 1, :] = -jnp.concatenate(parts, axis=1)
+
+    def body(f, carry):
+        rows_energy = e_ref[f, 0].T
+        occ_row = occ_ref[f * columns + lax.axis_index("ia")]
+        for b in range(columns):
+            occ_col = occ_ref[lax.axis_index("ja") * columns + b]
+            cols_energy = e_ref[f, 0, b : b + 1, :] - occ_col
+            denominator = (rows_energy[:, b : b + 1] - occ_row) + cols_energy
+            keep = inside_mask(counts_ref[f, 0, b], virtuals)
+            gain_ref[f, b] = jnp.where(keep, DAMPING * pl.reciprocal(denominator), 0.0)
+        return carry
+
+    lax.fori_loop(0, fragments, body, 0)
+
+
+def updated(f, b, amps, gain_ref, h_ref, p_ref):
+    residual = h_ref[b, f].astype(F32) + p_ref[b, f].T.astype(F32)
+    return ((1.0 - DAMPING) * amps.astype(F32) - gain_ref[f, b] * residual).astype(BF)
+
+
+def middle_kernel(
+    offset, inner, gain_ref, h_ref, p_ref, t_ref, c_ref,
+    tm_ref, x_ref, near_ref, far_ref,
+):
+    parity = lax.rem(lax.axis_index("ja"), 2)
+
+    def body(f, carry):
+        def amps(b):
+            value = updated(f + offset, b, t_ref[f + inner, b], gain_ref, h_ref, p_ref)
+            tm_ref[f, b] = value
+            return value
+
+        back_forms(f, parity, amps, lambda b: c_ref[f + inner, b], x_ref, near_ref, far_ref)
+        return carry
+
+    lax.fori_loop(0, x_ref.shape[0], body, 0)
+
+
+def last_kernel(gain_ref, h_ref, p_ref, *rest):
+    out_hbm, made_ref, sems = rest[-3:]
+    columns = made_ref.shape[1]
+
+    def store(f):
+        return pltpu.make_async_copy(made_ref.at[f], out_hbm.at[f, 0], sems.at[f])
+
+    offset = 0
+    for t_ref in rest[:-3]:
+
+        def body(f, carry, offset=offset, t_ref=t_ref):
+            for b in range(columns):
+                made_ref[f + offset, b] = updated(
+                    f + offset, b, t_ref[f, b], gain_ref, h_ref, p_ref
+                )
+            store(f + offset).start()
+            return carry
+
+        lax.fori_loop(0, t_ref.shape[0], body, 0)
+        offset += t_ref.shape[0]
+    for f in range(offset):
+        store(f).wait()
+
+
+def left_quads(amps, ints):
+    return (nn(amps, ints) * (1.0 / amps.shape[0])).astype(BF)
+
+
+def half_kernel(offset, inner, w_ref, t_ref, c_ref, k_ref, x_ref, near_ref, far_ref, *rest):
     h_ref, xf = rest[-2:]
     size, columns, virtuals = x_ref.shape[:3]
     lag = columns // 2
@@ -211,19 +216,19 @@
         for step in range(columns + 2 * lag):
             b = step
             if b < columns:
-                total = w_ref[(f + offset) * 2 * WIN, 0, b] * xf[b + WIN + window_shift(0)]
+                total = w_ref[0, (f + offset) * columns + b] * xf[b + WIN + window_shift(0)]
                 for s in range(1, 2 * WIN):
-                    total = total + w_ref[(f + offset) * 2 * WIN + s, 0, b] * xf[b + WIN + window_shift(s)]
+                    total = total + w_ref[s, (f + offset) * columns + b] * xf[b + WIN + window_shift(s)]
                 window[b] = total.astype(BF)
             b = step - lag
             if 0 <= b < columns:
-                left_proj[b] = tn(c_ref[f, b], window.pop(b)).astype(BF)
-                left_quad[b] = (nn(t_ref[f, b], k_ref[f + offset, b]) * (1.0 / virtuals)).astype(BF)
+                left_proj[b] = tn(c_ref[f + inner, b], window.pop(b)).astype(BF)
+                left_quad[b] = left_quads(t_ref[f, b], k_ref[f + offset, b])
             b = step - 2 * lag
             if 0 <= b:
                 joined = nn(
                     jnp.concatenate([left_quad.pop(b), left_proj.pop(b)], axis=1),
-                    jnp.concatenate([t_ref[f, b], c_ref[f, b]], axis=0),
+                    jnp.concatenate([t_ref[f, b], c_ref[f + inner, b]], axis=0),
                 )
                 h_ref[b, f + offset] = (0.5 * k_ref[f + offset, b].astype(F32) + joined).astype(BF)
         return carry
@@ -256,13 +261,12 @@
     amplitudes, coefficients, integrals, pno_energy, pno_counts, coupled, occ_fock, occ_energy
 ):
     fragments, _, columns, virtuals, _ = amplitudes.shape
-    size = fragments // GROUPS
+    size = fragments // 2
     pairs = size * columns
     matmul = 2 * virtuals**3 * pairs
     block = 2 * virtuals**2 * pairs
     listed = jnp.transpose(coupled, (0, 3, 1, 2)).reshape(fragments * 2 * WIN, 1, columns)
     counts = pno_counts
-    energies = near_core(pno_energy)
 
     peers = lax.axis_size("ja")
     near_pairs = [(i, i ^ 1) for i in range(peers)]
@@ -271,8 +275,10 @@
     def near_shape(*lead):
         return pltpu.VMEM((*lead, virtuals, virtuals), BF)
 
-    group = near_shape(size, columns)
-    back = [group, near_shape(size, WIN), near_shape(size, WIN)]
+    def back_shapes(n):
+        return [near_shape(n, m) for m in (columns, WIN, WIN)]
+
+    group, back = near_shape(size, columns), back_shapes(size)
 
     def first_steps():
         tm, c, raw_next, c_next, *made = pl.pallas_call(
@@ -302,56 +308,57 @@
             name="second",
         )(counts, near_core(raw_next), near_core(c_next), far(integrals))
         borders.append(exchange(made_next))
-        weights = pl.pallas_call(
-            weights_kernel,
-            in_specs=[VMEM, VMEM],
-            out_shape=jax.ShapeDtypeStruct(listed.shape, F32),
-            out_specs=VMEM,
-            compiler_params=params(),
-            cost_estimate=cost(0, block // 8),
-            name="weights",
-        )(*lax.optimization_barrier((listed, occ_fock, tm_next))[:2])
-        return [tm, tm_next], [c, c_next], k, [made[0], made_next[0]], borders, weights
+        gain, weights = pl.pallas_call(
+            gain_kernel,
+            in_specs=[SMEM] * 2 + [VMEM] * 3,
+            out_shape=[
+                pltpu.VMEM((fragments, columns, virtuals, virtuals), F32),
+                jax.ShapeDtypeStruct((2 * WIN, fragments * columns), F32),
+            ],
+            out_specs=[VMEM] * 2,
+            compiler_params=params(),
+            cost_estimate=cost(16 * virtuals**2 * pairs, 4 * block),
+            name="gain",
+        )(*lax.optimization_barrier((occ_energy, counts, pno_energy, listed, occ_fock, tm_next))[:5])
+        return [tm, tm_next], [c, c_next], k, [made[0], made_next[0]], borders, weights, gain
 
     def exchange(made):
-        return lax.ppermute(made[1], "ja", near_pairs), lax.ppermute(made[2], "ja", far_pairs)
-
-    def next_step(g, halves, partner, current, coefs):
+        from_far = lax.ppermute(made[2], "ja", far_pairs)
+        return lax.ppermute(made[1], "ja", near_pairs), from_far
+
+    def next_step(offset, n, gain, halves, partner, current, coefs):
         return pl.pallas_call(
-            partial(middle_kernel, g * size),
-            in_specs=[SMEM] * 2 + [VMEM] * 5,
-            out_shape=[group] + back,
+            partial(middle_kernel, offset, offset % size),
+            in_specs=[VMEM] * 5,
+            out_shape=[near_shape(n, columns)] + back_shapes(n),
             out_specs=[VMEM] * 4,
             compiler_params=params(),
-            cost_estimate=cost(2 * matmul, block),
+            cost_estimate=cost(2 * matmul * n // size, block),
             name="middle",
-        )(
-            occ_energy, counts, energies, near_core(halves), near_core(partner),
-            near_core(current[g]), near_core(coefs[g]),
-        )
-
-    def half_step(g, weights, current, coefs, ints, back_form, from_near, from_far, out):
-        operands = [current[g], coefs[g], ints, back_form, from_near, from_far]
+        )(*map(near_core, (gain, halves, partner, current[offset // size], coefs[offset // size])))
+
+    def half_step(offset, weights, amps, coefs, ints, back_form, border, out):
+        operands = [amps, coefs[offset // size], ints, back_form, *border]
         aliases = {}
         if out is not None:
             aliases = {len(operands) + 1: 0}
             operands.append(out)
         return pl.pallas_call(
-            partial(half_kernel, g * size),
+            partial(half_kernel, offset, offset % size),
             in_specs=[SMEM] + [VMEM] * len(operands),
             out_shape=near_shape(columns, fragments),
             out_specs=VMEM,
             scratch_shapes=[pltpu.VMEM((columns + 2 * WIN, virtuals, virtuals), F32)],
             input_output_aliases=aliases,
             compiler_params=params(),
-            cost_estimate=cost(4 * matmul, 2 * block),
+            cost_estimate=cost(4 * matmul * amps.shape[0] // size, 2 * block),
             name="half",
         )(weights, *map(near_core, operands))
 
-    def last_step(halves, partner, current):
+    def last_step(gain, halves, partner, current):
         return pl.pallas_call(
             last_kernel,
-            in_specs=[SMEM] * 2 + [VMEM] * (3 + GROUPS),
+            in_specs=[VMEM] * (3 + len(current)),
             out_shape=pltpu.HBM(amplitudes.shape, BF),
             out_specs=HBM,
             scratch_shapes=[
@@ -359,32 +366,35 @@
                 pltpu.SemaphoreType.DMA((fragments,)),
             ],
             compiler_params=params(),
-            cost_estimate=cost(0, 2 * GROUPS * block),
+            cost_estimate=cost(0, 4 * block),
             name="last",
         )(
-            occ_energy, counts, energies, near_core(halves), near_core(partner),
+            near_core(gain), near_core(halves), near_core(partner),
             *map(near_core, current),
         )
 
     halves = partner = None
     for sweep in range(ITERS):
+        offsets = [sum(GROUPS[sweep][:g]) for g in range(len(GROUPS[sweep]))]
         if sweep == 0:
-            current, coefs, ints, back_form, borders, weights = first_steps()
+            current, coefs, ints, back_form, borders, weights, gain = first_steps()
         else:
             new, back_form, borders = [], [], []
-            for g in range(GROUPS):
-                tm, *made = next_step(g, halves, partner, current, coefs)
+            for offset, n in zip(offsets, GROUPS[sweep], strict=True):
+                tm, *made = next_step(offset, n, gain, halves, partner, current, coefs)
                 borders.append(exchange(made))
                 new.append(tm)
                 back_form.append(made[0])
             current = new
         halves = None
-        for g in range(GROUPS):
-            halves = half_step(g, weights, current, coefs, ints, back_form[g], *borders[g], halves)
+        for g, offset in enumerate(offsets):
+            halves = half_step(
+                offset, weights, current[g], coefs, ints, back_form[g], borders[g], halves
+            )
         sent = halves.reshape(columns * fragments, 1, virtuals, virtuals)
         arrived = lax.all_to_all(sent, ("ia", "ja"), split_axis=0, concat_axis=0, tiled=True)
         partner = arrived.reshape(columns, fragments, virtuals, virtuals)
-    return last_step(halves, partner, current)
+    return last_step(gain, halves, partner, current)
 
 
 def solution(mesh):

time: 196 us -> 188 us (0.959)
  waiting for transfers between devices: 7.58 us -> 1.91 us
  Pallas kernels: 54.1 us -> 48.6 us
  starting transfers between devices: 14.9 us -> 17.7 us
    ppermute x8 -> x10, waiting for transfers between devices: 7.58 us -> 1.91 us  [the longest x5 1.89 us: exchange(): from_far = lax.ppermute(made[2], 'ja', far_pairs)]
    pallas_call x8 -> x10, Pallas kernels: 46.6 us -> 41.1 us  [the longest x5 26.8 us: half_step(): pl.pallas_call(partial(half_kernel, offset, offset % size), in_specs=[SME...]
    ppermute x8 -> x10, starting transfers between devices: 14.9 us -> 17.7 us  [the longest x5 15 us: exchange(): from_far = lax.ppermute(made[2], 'ja', far_pairs)]
  transfers between devices with their start and end apart: 8 -> 10, of which waited for: 4 -> 2; matrix products, arithmetic and copies ran while one was open for 0% -> 0% of each run, Pallas kernels for 12% -> 15%
where the time goes in v3:
time: 188 us
  blocking collectives  120 us (64%)
  Pallas kernels  48.6 us (26%)
  starting transfers between devices  17.7 us (9%)
  waiting for transfers between devices  1.91 us (1%)
    all_to_all x2, blocking collectives, on_device(): lax.all_to_all(sent, ('ia', 'ja'), split_axis=0, concat_axis=0, tiled=True)  120 us
    pallas_call x5, Pallas kernels, half_step(): pl.pallas_call(partial(half_kernel, offset, offset % size), in_specs=[SME...  26.8 us
    ppermute x5, starting transfers between devices, exchange(): from_far = lax.ppermute(made[2], 'ja', far_pairs)  15 us
    pallas_call x3, Pallas kernels, next_step(): pl.pallas_call(partial(middle_kernel, offset, offset % size), in_specs=[V...  6.18 us
    pallas_call x1, Pallas kernels, first_steps(): pl.pallas_call(gain_kernel, in_specs=[SMEM] * 2 + [VMEM] * 3, out_shape=[...  4.72 us
    pallas_call x1, Pallas kernels, first_steps(): pl.pallas_call(start_kernel, in_specs=[HBM, HBM, HBM], out_shape=[group]...  4.1 us
  transfers between devices with their start and end apart: 10, of which 2 were waited for; matrix products, arithmetic and copies ran while one was open for 0% of the time, Pallas kernels for 15%

profile of v3, /device:TPU:1, one launch (start us, length us, event | category | flops | bytes accessed | tf_op | source)
XLA Modules:
  0.0 188.2 jit_solution(12492819142570746026)
XLA Ops:
  0.0 4.1 %start.1 = (bf16[4,16,128,128]{3,2,1,0:T(8,128)(2,1)S(1)}, bf16[4,16,128,128]{3,2,1,0:T(8,128)(2,1)S(1)}, bf16[4,16,128,128]{3,2,1,0:T(8,128)(2,1)S(1)}, bf16[4,...) custom-call(s32[8,1,16]{2,1,0:T(1,128)} %counts_ref.2, ...), custom_call_target="tpu_custom_call" | custom-call | flops 536870912 | bytes 8388608 | tf_op jit(solution)/shard_map/start/pallas_call | solution.py:284
  4.1 1.5 collective-permute-start.2
  5.6 3.2 %collective-permute-start.3 = (bf16[4,6,128,128]{3,2,1,0:T(8,128)(2,1)S(1)}, bf16[4,6,128,128]{3,2,1,0:T(8,128)(2,1)S(1)}, u32[]{:S(2)}, u32[]{:S(2)}) collective-permute-start(bf16[4,6,128,128]{3,2,1,0:T(8,128)(2,1)S(1)} %get-tuple-element.54), channel_id=1, source_target_pairs={{1,2},{2,1},{3,4},{4,3},{5,6},{6,5},{9,10},{10,9},{11,12},{12,11},... | collective-permute-start | bytes 2359304 | tf_op jit(solution)/shard_map/ppermute | solution.py:326
  8.8 0.0 copy-start
  8.8 0.0 copy-start.1
  8.8 0.0 copy-start.2
  8.9 0.0 copy-start.4
  8.9 3.4 %second.1 = (bf16[4,16,128,128]{3,2,1,0:T(8,128)(2,1)S(1)}, bf16[8,16,128,128]{3,2,1,0:T(8,128)(2,1)S(1)}, bf16[4,16,128,128]{3,2,1,0:T(8,128)(2,1)S(1)}, bf16[4...) custom-call(s32[8,1,16]{2,1,0:T(1,128)S(1)} %copy-done.3, ...), custom_call_target="tpu_custom_call" | custom-call | flops 536870912 | bytes 4194304 | tf_op jit(solution)/shard_map/second/pallas_call | solution.py:300
  12.3 0.1 collective-permute-start
  12.4 3.6 %collective-permute-start.1 = (bf16[4,6,128,128]{3,2,1,0:T(8,128)(2,1)S(1)}, bf16[4,6,128,128]{3,2,1,0:T(8,128)(2,1)S(1)}, u32[]{:S(2)}, u32[]{:S(2)}) collective-permute-start(bf16[4,6,128,128]{3,2,1,0:T(8,128)(2,1)S(1)} %get-tuple-element.49), channel_id=1, source_target_pairs={{1,2},{2,1},{3,4},{4,3},{5,6},{6,5},{9,10},{10,9},{11,12},{12,11},... | collective-permute-start | bytes 2359304 | tf_op jit(solution)/shard_map/ppermute | solution.py:326
  16.0 4.7 %gain.1 = (f32[8,16,128,128]{3,2,1,0:T(8,128)S(1)}, f32[12,128]{1,0:T(8,128)S(1)}) custom-call(f32[128]{0:T(128)S(1)} %copy-done.4, s32[8,1,16]{2,1,0:T(1,128)S(1)} %copy-done.3, f32[8,1,16,128]{3,2,1,0:T(8,128)S(1)} %copy-done, s32[96,1,16]{2,1,0:T(1,128)S(1)} %bitcast.17, f32[128,128]{1,0:T(8,128)S(1)} %copy-done.1), custom_call_target="tpu_custom_call" | custom-call | flops 16777216 | bytes 8388608 | tf_op jit(solution)/shard_map/gain/pallas_call | solution.py:311
  20.7 6.4 %half.5.rest_0_ = bf16[16,8,128,128]{3,2,1,0:T(8,128)(2,1)S(1)} custom-call(f32[12,128]{1,0:T(8,128)S(1)} %get-tuple-element.45.w_ref, bf16[4,16,128,128]{3,2,1,0:T(8,128)(2,1)S(1)} %get-tuple-element.50.t_ref, bf16[4,16,128,128]{3,2,1,0:T(8,128)(2,1)S(1)} %get-tuple-element.51.c_ref, bf16[8,16,128,128]{3,2,1,0:T(8,128)(2,1)S(1)} %get-tuple-element.46.k_ref, ...), custom_call_target="tpu_custom_call" | custom-call | flops 1073741824 | bytes 4194304 | tf_op jit(solution)/shard_map/half/pallas_call | solution.py:346
  27.2 0.2 collective-permute-done.1.far_ref
  27.3 6.6 %half.6.h_ref = bf16[16,8,128,128]{3,2,1,0:T(8,128)(2,1)S(1)} custom-call(f32[12,128]{1,0:T(8,128)S(1)} %get-tuple-element.45.w_ref, bf16[4,16,128,128]{3,2,1,0:T(8,128)(2,1)S(1)} %get-tuple-element.38.t_ref, bf16[4,16,128,128]{3,2,1,0:T(8,128)(2,1)S(1)} %get-tuple-element.37.c_ref, ...), custom_call_target="tpu_custom_call", output_to_operand_aliasing={{}: (7, {})} | custom-call | flops 1073741824 | bytes 4194304 | tf_op jit(solution)/shard_map/half/pallas_call | solution.py:346
  33.9 63.2 %all_to_all.10 = bf16[128,1,128,128]{3,2,1,0:T(8,128)(2,1)S(1)} all-to-all(bf16[128,1,128,128]{3,2,1,0:T(8,128)(2,1)S(1)} %bitcast.11), channel_id=1, replica_groups=mesh['ia'=16,'ja'=8] {'ia','ja'}, dimensions={0} | all-to-all | bytes 8388608 | tf_op jit(solution)/shard_map/all_to_all | solution.py:395
  97.1 3.0 %middle.5 = (bf16[4,16,128,128]{3,2,1,0:T(8,128)(2,1)S(1)}, bf16[4,16,128,128]{3,2,1,0:T(8,128)(2,1)S(1)}, bf16[4,6,128,128]{3,2,1,0:T(8,128)(2,1)S(1)}, bf16[4,6,128,128]{3,2,1,0:T(8,128)(2,1)S(1)}) custom-call(f32[8,16,128,128]{3,2,1,0:T(8,128)S(1)} %get-tuple-element.44.gain_ref, bf16[16,8,128,128]{3,2,1,0:T(8,128)(2,1)S(1)} %half.6.h_ref, ...), custom_call_target="tpu_custom_call" | custom-call | flops 536870912 | bytes 2097152 | tf_op jit(solution)/shard_map/middle/pallas_call | solution.py:330
  100.1 0.9 collective-permute-start.8
  101.0 2.0 %collective-permute-start.9 = (bf16[4,6,128,128]{3,2,1,0:T(8,128)(2,1)S(1)}, bf16[4,6,128,128]{3,2,1,0:T(8,128)(2,1)S(1)}, u32[]{:S(2)}, u32[]{:S(2)}) collective-permute-start(bf16[4,6,128,128]{3,2,1,0:T(8,128)(2,1)S(1)} %get-tuple-element.66), channel_id=1, source_target_pairs={{1,2},{2,1},{3,4},{4,3},{5,6},{6,5},{9,10},{10,9},{11,12},{12,11},... | collective-permute-start | bytes 2359304 | tf_op jit(solution)/shard_map/ppermute | solution.py:326
  103.1 1.6 middle.4
  104.7 0.1 collective-permute-start.6
  104.8 3.5 %collective-permute-start.7 = (bf16[2,6,128,128]{3,2,1,0:T(8,128)(2,1)S(1)}, bf16[2,6,128,128]{3,2,1,0:T(8,128)(2,1)S(1)}, u32[]{:S(2)}, u32[]{:S(2)}) collective-permute-start(bf16[2,6,128,128]{3,2,1,0:T(8,128)(2,1)S(1)} %get-tuple-element.62), channel_id=1, source_target_pairs={{1,2},{2,1},{3,4},{4,3},{5,6},{6,5},{9,10},{10,9},{11,12},{12,11},... | collective-permute-start | bytes 1179656 | tf_op jit(solution)/shard_map/ppermute | solution.py:326
  108.3 1.6 middle.3
  109.9 0.1 collective-permute-start.4
  110.0 2.7 %collective-permute-start.5 = (bf16[2,6,128,128]{3,2,1,0:T(8,128)(2,1)S(1)}, bf16[2,6,128,128]{3,2,1,0:T(8,128)(2,1)S(1)}, u32[]{:S(2)}, u32[]{:S(2)}) collective-permute-start(bf16[2,6,128,128]{3,2,1,0:T(8,128)(2,1)S(1)} %get-tuple-element.58), channel_id=1, source_target_pairs={{1,2},{2,1},{3,4},{4,3},{5,6},{6,5},{9,10},{10,9},{11,12},{12,11},... | collective-permute-start | bytes 1179656 | tf_op jit(solution)/shard_map/ppermute | solution.py:326
  112.6 1.7 collective-permute-done.9.far_ref
  114.3 6.6 %half.7.rest_0_ = bf16[16,8,128,128]{3,2,1,0:T(8,128)(2,1)S(1)} custom-call(f32[12,128]{1,0:T(8,128)S(1)} %get-tuple-element.45.w_ref, bf16[4,16,128,128]{3,2,1,0:T(8,128)(2,1)S(1)} %get-tuple-element.63.t_ref.rest_0_, bf16[4,16,128,128]{3,2,1,0:T(8,128)(2,1)S(1)} %get-tuple-element.51.c_ref, bf16[8,16,128,128]{3,2,1,0:T(8,128)(2,1)S(1)} %get-tuple-element.46.k_ref, ...), custom_call_target="tpu_custom_call" | custom-call | flops 1073741824 | bytes 4194304 | tf_op jit(solution)/shard_map/half/pallas_call | solution.py:346
  121.0 0.0 collective-permute-done.7.far_ref
  121.0 3.5 %half.8.rest_0_ = bf16[16,8,128,128]{3,2,1,0:T(8,128)(2,1)S(1)} custom-call(f32[12,128]{1,0:T(8,128)S(1)} %get-tuple-element.45.w_ref, bf16[2,16,128,128]{3,2,1,0:T(8,128)(2,1)S(1)} %get-tuple-element.59.t_ref.rest_1_, bf16[4,16,128,128]{3,2,1,0:T(8,128)(2,1)S(1)} %get-tuple-element.37.c_ref, ...), custom_call_target="tpu_custom_call", output_to_operand_aliasing={{}: (7, {})} | custom-call | flops 536870912 | bytes 4194304 | tf_op jit(solution)/shard_map/half/pallas_call | solution.py:346
  124.6 0.0 collective-permute-done.5.far_ref
  124.6 3.7 %half.9.h_ref = bf16[16,8,128,128]{3,2,1,0:T(8,128)(2,1)S(1)} custom-call(f32[12,128]{1,0:T(8,128)S(1)} %get-tuple-element.45.w_ref, bf16[2,16,128,128]{3,2,1,0:T(8,128)(2,1)S(1)} %get-tuple-element.55.t_ref.rest_2_, bf16[4,16,128,128]{3,2,1,0:T(8,128)(2,1)S(1)} %get-tuple-element.37.c_ref, ...), custom_call_target="tpu_custom_call", output_to_operand_aliasing={{}: (7, {})} | custom-call | flops 536870912 | bytes 4194304 | tf_op jit(solution)/shard_map/half/pallas_call | solution.py:346
  128.2 56.4 %all_to_all.11 = bf16[128,1,128,128]{3,2,1,0:T(8,128)(2,1)S(1)} all-to-all(bf16[128,1,128,128]{3,2,1,0:T(8,128)(2,1)S(1)} %bitcast.12), channel_id=1, replica_groups=mesh['ia'=16,'ja'=8] {'ia','ja'}, dimensions={0} | all-to-all | bytes 8388608 | tf_op jit(solution)/shard_map/all_to_all | solution.py:395
  184.6 3.4 %last.1 = bf16[8,1,16,128,128]{4,3,2,1,0:T(8,128)(2,1)} custom-call(f32[8,16,128,128]{3,2,1,0:T(8,128)S(1)} %get-tuple-element.44.gain_ref, bf16[16,8,128,128]{3,2,1,0:T(8,128)(2,1)S(1)} %half.9.h_ref, bf16[16,8,128,128]{3,2,1,0:T(8,128)(2,1)S(1)} %bitcast.16, bf16[4,16,128,128]{3,2,1,0:T(8,128)(2,1)S(1)} %get-tuple-element.63.t_ref.rest_0_, ...), custom_call_target="tpu_custom_call" | custom-call | bytes 8388608 | tf_op jit(solution)/shard_map/last/pallas_call | solution.py:359
  (12 shorter events, 0.0 us)
Async XLA Ops:
  0.0 8.8 %copy-start.3 = (s32[8,1,16]{2,1,0:T(1,128)S(1)}, s32[8,1,16]{2,1,0:T(1,128)}, u32[]{:S(2)}) copy-start(s32[8,1,16]{2,1,0:T(1,128)} %counts_ref.2) | copy-start | bytes 1540
  4.1 16.6 %collective-permute-start.2 = (bf16[4,6,128,128]{3,2,1,0:T(8,128)(2,1)S(1)}, bf16[4,6,128,128]{3,2,1,0:T(8,128)(2,1)S(1)}, u32[]{:S(2)}, u32[]{:S(2)}) collective-permute-start(bf16[4,6,128,128]{3,2,1,0:T(8,128)(2,1)S(1)} %get-tuple-element.53), channel_id=1, source_target_pairs={{0,1},{1,0},{2,3},{3,2},{4,5},{5,4},{6,7},{7,6},{8,9},{9,8},{10,11... | collective-permute-start | bytes 2359304 | tf_op jit(solution)/shard_map/ppermute | solution.py:327
  5.6 15.1 %collective-permute-start.3 = (bf16[4,6,128,128]{3,2,1,0:T(8,128)(2,1)S(1)}, bf16[4,6,128,128]{3,2,1,0:T(8,128)(2,1)S(1)}, u32[]{:S(2)}, u32[]{:S(2)}) collective-permute-start(bf16[4,6,128,128]{3,2,1,0:T(8,128)(2,1)S(1)} %get-tuple-element.54), channel_id=1, source_target_pairs={{1,2},{2,1},{3,4},{4,3},{5,6},{6,5},{9,10},{10,9},{11,12},{12,11},... | collective-permute-start | bytes 2359304 | tf_op jit(solution)/shard_map/ppermute | solution.py:326
  8.8 7.1 %copy-start = (f32[8,1,16,128]{3,2,1,0:T(8,128)S(1)}, f32[8,1,16,128]{3,2,1,0:T(8,128)}, u32[]{:S(2)}) copy-start(f32[8,1,16,128]{3,2,1,0:T(8,128)} %e_ref) | copy-start | bytes 196612
  8.8 7.1 %copy-start.1 = (f32[128,128]{1,0:T(8,128)S(1)}, f32[128,128]{1,0:T(8,128)}, u32[]{:S(2)}) copy-start(f32[128,128]{1,0:T(8,128)} %fock_ref) | copy-start | bytes 196612
  8.8 7.1 %copy-start.2 = (s32[8,1,16,12]{2,1,3,0:T(1,128)S(1)}, s32[8,1,16,12]{2,1,3,0:T(1,128)}, u32[]{:S(2)}) copy-start(s32[8,1,16,12]{2,1,3,0:T(1,128)} %param.13) | copy-start | bytes 18436
  8.9 7.1 %copy-start.4 = (f32[128]{0:T(128)S(1)}, f32[128]{0:T(128)}, u32[]{:S(2)}) copy-start(f32[128]{0:T(128)} %occ_ref) | copy-start | bytes 1540
  12.3 14.9 %collective-permute-start = (bf16[4,6,128,128]{3,2,1,0:T(8,128)(2,1)S(1)}, bf16[4,6,128,128]{3,2,1,0:T(8,128)(2,1)S(1)}, u32[]{:S(2)}, u32[]{:S(2)}) collective-permute-start(bf16[4,6,128,128]{3,2,1,0:T(8,128)(2,1)S(1)} %get-tuple-element.48), channel_id=1, source_target_pairs={{0,1},{1,0},{2,3},{3,2},{4,5},{5,4},{6,7},{7,6},{8,9},{9,8},{10,11... | collective-permute-start | bytes 2359304 | tf_op jit(solution)/shard_map/ppermute | solution.py:327
  12.4 15.0 %collective-permute-start.1 = (bf16[4,6,128,128]{3,2,1,0:T(8,128)(2,1)S(1)}, bf16[4,6,128,128]{3,2,1,0:T(8,128)(2,1)S(1)}, u32[]{:S(2)}, u32[]{:S(2)}) collective-permute-start(bf16[4,6,128,128]{3,2,1,0:T(8,128)(2,1)S(1)} %get-tuple-element.49), channel_id=1, source_target_pairs={{1,2},{2,1},{3,4},{4,3},{5,6},{6,5},{9,10},{10,9},{11,12},{12,11},... | collective-permute-start | bytes 2359304 | tf_op jit(solution)/shard_map/ppermute | solution.py:326
  100.1 9.8 %collective-permute-start.8 = (bf16[4,6,128,128]{3,2,1,0:T(8,128)(2,1)S(1)}, bf16[4,6,128,128]{3,2,1,0:T(8,128)(2,1)S(1)}, u32[]{:S(2)}, u32[]{:S(2)}) collective-permute-start(bf16[4,6,128,128]{3,2,1,0:T(8,128)(2,1)S(1)} %get-tuple-element.65), channel_id=1, source_target_pairs={{0,1},{1,0},{2,3},{3,2},{4,5},{5,4},{6,7},{7,6},{8,9},{9,8},{10,11... | collective-permute-start | bytes 2359304 | tf_op jit(solution)/shard_map/ppermute | solution.py:327
  101.0 13.3 %collective-permute-start.9 = (bf16[4,6,128,128]{3,2,1,0:T(8,128)(2,1)S(1)}, bf16[4,6,128,128]{3,2,1,0:T(8,128)(2,1)S(1)}, u32[]{:S(2)}, u32[]{:S(2)}) collective-permute-start(bf16[4,6,128,128]{3,2,1,0:T(8,128)(2,1)S(1)} %get-tuple-element.66), channel_id=1, source_target_pairs={{1,2},{2,1},{3,4},{4,3},{5,6},{6,5},{9,10},{10,9},{11,12},{12,11},... | collective-permute-start | bytes 2359304 | tf_op jit(solution)/shard_map/ppermute | solution.py:326
  104.7 16.3 %collective-permute-start.6 = (bf16[2,6,128,128]{3,2,1,0:T(8,128)(2,1)S(1)}, bf16[2,6,128,128]{3,2,1,0:T(8,128)(2,1)S(1)}, u32[]{:S(2)}, u32[]{:S(2)}) collective-permute-start(bf16[2,6,128,128]{3,2,1,0:T(8,128)(2,1)S(1)} %get-tuple-element.61), channel_id=1, source_target_pairs={{0,1},{1,0},{2,3},{3,2},{4,5},{5,4},{6,7},{7,6},{8,9},{9,8},{10,11... | collective-permute-start | bytes 1179656 | tf_op jit(solution)/shard_map/ppermute | solution.py:327
  104.8 16.2 %collective-permute-start.7 = (bf16[2,6,128,128]{3,2,1,0:T(8,128)(2,1)S(1)}, bf16[2,6,128,128]{3,2,1,0:T(8,128)(2,1)S(1)}, u32[]{:S(2)}, u32[]{:S(2)}) collective-permute-start(bf16[2,6,128,128]{3,2,1,0:T(8,128)(2,1)S(1)} %get-tuple-element.62), channel_id=1, source_target_pairs={{1,2},{2,1},{3,4},{4,3},{5,6},{6,5},{9,10},{10,9},{11,12},{12,11},... | collective-permute-start | bytes 1179656 | tf_op jit(solution)/shard_map/ppermute | solution.py:326
  109.9 14.7 %collective-permute-start.4 = (bf16[2,6,128,128]{3,2,1,0:T(8,128)(2,1)S(1)}, bf16[2,6,128,128]{3,2,1,0:T(8,128)(2,1)S(1)}, u32[]{:S(2)}, u32[]{:S(2)}) collective-permute-start(bf16[2,6,128,128]{3,2,1,0:T(8,128)(2,1)S(1)} %get-tuple-element.57), channel_id=1, source_target_pairs={{0,1},{1,0},{2,3},{3,2},{4,5},{5,4},{6,7},{7,6},{8,9},{9,8},{10,11... | collective-permute-start | bytes 1179656 | tf_op jit(solution)/shard_map/ppermute | solution.py:327
  110.0 14.6 %collective-permute-start.5 = (bf16[2,6,128,128]{3,2,1,0:T(8,128)(2,1)S(1)}, bf16[2,6,128,128]{3,2,1,0:T(8,128)(2,1)S(1)}, u32[]{:S(2)}, u32[]{:S(2)}) collective-permute-start(bf16[2,6,128,128]{3,2,1,0:T(8,128)(2,1)S(1)} %get-tuple-element.58), channel_id=1, source_target_pairs={{1,2},{2,1},{3,4},{4,3},{5,6},{6,5},{9,10},{10,9},{11,12},{12,11},... | collective-permute-start | bytes 1179656 | tf_op jit(solution)/shard_map/ppermute | solution.py:326

commit v4 on v3

--- a/solution.py
+++ b/solution.py
@@ -135,7 +135,7 @@
         band = jnp.where(rows == cols + window_shift(s), fock_ref[...], 0.0)
         band = pltpu.roll(jnp.sum(band, axis=0, keepdims=True), turn, 1)[:, :columns]
         parts = [coupled_ref[f * slots + s].astype(F32) * band for f in range(fragments)]
-        w_ref[s : s + 1, :] = -jnp.concatenate(parts, axis=1)
+        w_ref[s : s + 1, :] = -virtuals * jnp.concatenate(parts, axis=1)
 
     def body(f, carry):
         rows_energy = e_ref[f, 0].T
@@ -145,7 +145,7 @@
             cols_energy = e_ref[f, 0, b : b + 1, :] - occ_col
             denominator = (rows_energy[:, b : b + 1] - occ_row) + cols_energy
             keep = inside_mask(counts_ref[f, 0, b], virtuals)
-            gain_ref[f, b] = jnp.where(keep, DAMPING * pl.reciprocal(denominator), 0.0)
+            gain_ref[f, b] = jnp.where(keep, (DAMPING / virtuals) * pl.reciprocal(denominator), 0.0)
         return carry
 
     lax.fori_loop(0, fragments, body, 0)
@@ -196,10 +196,6 @@
         offset += t_ref.shape[0]
     for f in range(offset):
         store(f).wait()
-
-
-def left_quads(amps, ints):
-    return (nn(amps, ints) * (1.0 / amps.shape[0])).astype(BF)
 
 
 def half_kernel(offset, inner, w_ref, t_ref, c_ref, k_ref, x_ref, near_ref, far_ref, *rest):
@@ -222,15 +218,13 @@
                 window[b] = total.astype(BF)
             b = step - lag
             if 0 <= b < columns:
-                left_proj[b] = tn(c_ref[f + inner, b], window.pop(b)).astype(BF)
-                left_quad[b] = left_quads(t_ref[f, b], k_ref[f + offset, b])
+                left_proj[b] = tn(window.pop(b), c_ref[f + inner, b]).astype(BF)
+                left_quad[b] = nn(t_ref[f, b], k_ref[f + offset, b]).astype(BF)
             b = step - 2 * lag
             if 0 <= b:
-                joined = nn(
-                    jnp.concatenate([left_quad.pop(b), left_proj.pop(b)], axis=1),
-                    jnp.concatenate([t_ref[f, b], c_ref[f + inner, b]], axis=0),
-                )
-                h_ref[b, f + offset] = (0.5 * k_ref[f + offset, b].astype(F32) + joined).astype(BF)
+                joined = tn(left_proj.pop(b), c_ref[f + inner, b]) + nn(left_quad.pop(b), t_ref[f, b])
+                scaled = (0.5 * virtuals) * k_ref[f + offset, b].astype(F32)
+                h_ref[b, f + offset] = (scaled + joined).astype(BF)
         return carry
 
     lax.fori_loop(0, size, body, 0)

time: 188 us -> 188 us (level)
  no operation moved by 1% of the time
where the time goes in v4:
time: 188 us; the launch traced here: 187 us
  blocking collectives  120 us (64%)
  Pallas kernels  47.7 us (25%)
  starting transfers between devices  17.7 us (9%)
  waiting for transfers between devices  2.12 us (1%)
    all_to_all x2, blocking collectives, on_device(): lax.all_to_all(sent, ('ia', 'ja'), split_axis=0, concat_axis=0, tiled=True)  120 us
    pallas_call x5, Pallas kernels, half_step(): pl.pallas_call(partial(half_kernel, offset, offset % size), in_specs=[SME...  25.9 us
    ppermute x5, starting transfers between devices, exchange(): from_far = lax.ppermute(made[2], 'ja', far_pairs)  15 us
    pallas_call x3, Pallas kernels, next_step(): pl.pallas_call(partial(middle_kernel, offset, offset % size), in_specs=[V...  6.18 us
    pallas_call x1, Pallas kernels, first_steps(): pl.pallas_call(gain_kernel, in_specs=[SMEM] * 2 + [VMEM] * 3, out_shape=[...  4.72 us
    pallas_call x1, Pallas kernels, first_steps(): pl.pallas_call(start_kernel, in_specs=[HBM, HBM, HBM], out_shape=[group]...  4.1 us
  transfers between devices with their start and end apart: 10, of which 2 were waited for; matrix products, arithmetic and copies ran while one was open for 0% of the time, Pallas kernels for 15%

profile of v4, /device:TPU:1, one launch (start us, length us, event | category | flops | bytes accessed | tf_op | source)
XLA Modules:
  0.0 187.5 jit_solution(16890669756750514680)
XLA Ops:
  0.0 4.1 %start.1 = (bf16[4,16,128,128]{3,2,1,0:T(8,128)(2,1)S(1)}, bf16[4,16,128,128]{3,2,1,0:T(8,128)(2,1)S(1)}, bf16[4,16,128,128]{3,2,1,0:T(8,128)(2,1)S(1)}, bf16[4,...) custom-call(s32[8,1,16]{2,1,0:T(1,128)} %counts_ref.2, ...), custom_call_target="tpu_custom_call" | custom-call | flops 536870912 | bytes 8388608 | tf_op jit(solution)/shard_map/start/pallas_call | solution.py:278
  4.1 1.5 collective-permute-start.2
  5.6 3.2 %collective-permute-start.3 = (bf16[4,6,128,128]{3,2,1,0:T(8,128)(2,1)S(1)}, bf16[4,6,128,128]{3,2,1,0:T(8,128)(2,1)S(1)}, u32[]{:S(2)}, u32[]{:S(2)}) collective-permute-start(bf16[4,6,128,128]{3,2,1,0:T(8,128)(2,1)S(1)} %get-tuple-element.54), channel_id=1, source_target_pairs={{1,2},{2,1},{3,4},{4,3},{5,6},{6,5},{9,10},{10,9},{11,12},{12,11},... | collective-permute-start | bytes 2359304 | tf_op jit(solution)/shard_map/ppermute | solution.py:320
  8.8 0.0 copy-start
  8.8 0.0 copy-start.1
  8.8 0.0 copy-start.2
  8.9 0.0 copy-start.4
  8.9 3.4 %second.1 = (bf16[4,16,128,128]{3,2,1,0:T(8,128)(2,1)S(1)}, bf16[8,16,128,128]{3,2,1,0:T(8,128)(2,1)S(1)}, bf16[4,16,128,128]{3,2,1,0:T(8,128)(2,1)S(1)}, bf16[4...) custom-call(s32[8,1,16]{2,1,0:T(1,128)S(1)} %copy-done.3, ...), custom_call_target="tpu_custom_call" | custom-call | flops 536870912 | bytes 4194304 | tf_op jit(solution)/shard_map/second/pallas_call | solution.py:294
  12.3 0.1 collective-permute-start
  12.4 3.6 %collective-permute-start.1 = (bf16[4,6,128,128]{3,2,1,0:T(8,128)(2,1)S(1)}, bf16[4,6,128,128]{3,2,1,0:T(8,128)(2,1)S(1)}, u32[]{:S(2)}, u32[]{:S(2)}) collective-permute-start(bf16[4,6,128,128]{3,2,1,0:T(8,128)(2,1)S(1)} %get-tuple-element.49), channel_id=1, source_target_pairs={{1,2},{2,1},{3,4},{4,3},{5,6},{6,5},{9,10},{10,9},{11,12},{12,11},... | collective-permute-start | bytes 2359304 | tf_op jit(solution)/shard_map/ppermute | solution.py:320
  16.0 4.7 %gain.1 = (f32[8,16,128,128]{3,2,1,0:T(8,128)S(1)}, f32[12,128]{1,0:T(8,128)S(1)}) custom-call(f32[128]{0:T(128)S(1)} %copy-done.4, s32[8,1,16]{2,1,0:T(1,128)S(1)} %copy-done.3, f32[8,1,16,128]{3,2,1,0:T(8,128)S(1)} %copy-done, s32[96,1,16]{2,1,0:T(1,128)S(1)} %bitcast.17, f32[128,128]{1,0:T(8,128)S(1)} %copy-done.1), custom_call_target="tpu_custom_call" | custom-call | flops 16777216 | bytes 8388608 | tf_op jit(solution)/shard_map/gain/pallas_call | solution.py:305
  20.7 6.2 %half.5.rest_0_ = bf16[16,8,128,128]{3,2,1,0:T(8,128)(2,1)S(1)} custom-call(f32[12,128]{1,0:T(8,128)S(1)} %get-tuple-element.45.w_ref, bf16[4,16,128,128]{3,2,1,0:T(8,128)(2,1)S(1)} %get-tuple-element.50.t_ref, bf16[4,16,128,128]{3,2,1,0:T(8,128)(2,1)S(1)} %get-tuple-element.51.c_ref, bf16[8,16,128,128]{3,2,1,0:T(8,128)(2,1)S(1)} %get-tuple-element.46.k_ref, ...), custom_call_target="tpu_custom_call" | custom-call | flops 1073741824 | bytes 4194304 | tf_op jit(solution)/shard_map/half/pallas_call | solution.py:340
  26.9 0.0 collective-permute-done.near_ref
  26.9 0.4 collective-permute-done.1.far_ref
  27.3 6.3 %half.6.h_ref = bf16[16,8,128,128]{3,2,1,0:T(8,128)(2,1)S(1)} custom-call(f32[12,128]{1,0:T(8,128)S(1)} %get-tuple-element.45.w_ref, bf16[4,16,128,128]{3,2,1,0:T(8,128)(2,1)S(1)} %get-tuple-element.38.t_ref, bf16[4,16,128,128]{3,2,1,0:T(8,128)(2,1)S(1)} %get-tuple-element.37.c_ref, ...), custom_call_target="tpu_custom_call", output_to_operand_aliasing={{}: (7, {})} | custom-call | flops 1073741824 | bytes 4194304 | tf_op jit(solution)/shard_map/half/pallas_call | solution.py:340
  33.7 63.2 %all_to_all.10 = bf16[128,1,128,128]{3,2,1,0:T(8,128)(2,1)S(1)} all-to-all(bf16[128,1,128,128]{3,2,1,0:T(8,128)(2,1)S(1)} %bitcast.11), channel_id=1, replica_groups=mesh['ia'=16,'ja'=8] {'ia','ja'}, dimensions={0} | all-to-all | bytes 8388608 | tf_op jit(solution)/shard_map/all_to_all | solution.py:389
  96.9 3.0 %middle.5 = (bf16[4,16,128,128]{3,2,1,0:T(8,128)(2,1)S(1)}, bf16[4,16,128,128]{3,2,1,0:T(8,128)(2,1)S(1)}, bf16[4,6,128,128]{3,2,1,0:T(8,128)(2,1)S(1)}, bf16[4,6,128,128]{3,2,1,0:T(8,128)(2,1)S(1)}) custom-call(f32[8,16,128,128]{3,2,1,0:T(8,128)S(1)} %get-tuple-element.44.gain_ref, bf16[16,8,128,128]{3,2,1,0:T(8,128)(2,1)S(1)} %half.6.h_ref, ...), custom_call_target="tpu_custom_call" | custom-call | flops 536870912 | bytes 2097152 | tf_op jit(solution)/shard_map/middle/pallas_call | solution.py:324
  99.9 0.9 collective-permute-start.8
  100.8 2.0 %collective-permute-start.9 = (bf16[4,6,128,128]{3,2,1,0:T(8,128)(2,1)S(1)}, bf16[4,6,128,128]{3,2,1,0:T(8,128)(2,1)S(1)}, u32[]{:S(2)}, u32[]{:S(2)}) collective-permute-start(bf16[4,6,128,128]{3,2,1,0:T(8,128)(2,1)S(1)} %get-tuple-element.66), channel_id=1, source_target_pairs={{1,2},{2,1},{3,4},{4,3},{5,6},{6,5},{9,10},{10,9},{11,12},{12,11},... | collective-permute-start | bytes 2359304 | tf_op jit(solution)/shard_map/ppermute | solution.py:320
  102.9 1.6 middle.4
  104.4 0.1 collective-permute-start.6
  104.5 3.5 %collective-permute-start.7 = (bf16[2,6,128,128]{3,2,1,0:T(8,128)(2,1)S(1)}, bf16[2,6,128,128]{3,2,1,0:T(8,128)(2,1)S(1)}, u32[]{:S(2)}, u32[]{:S(2)}) collective-permute-start(bf16[2,6,128,128]{3,2,1,0:T(8,128)(2,1)S(1)} %get-tuple-element.62), channel_id=1, source_target_pairs={{1,2},{2,1},{3,4},{4,3},{5,6},{6,5},{9,10},{10,9},{11,12},{12,11},... | collective-permute-start | bytes 1179656 | tf_op jit(solution)/shard_map/ppermute | solution.py:320
  108.1 1.6 middle.3
  109.6 0.1 collective-permute-start.4
  109.7 0.0 collective-permute-done.8.near_ref
  109.7 2.7 %collective-permute-start.5 = (bf16[2,6,128,128]{3,2,1,0:T(8,128)(2,1)S(1)}, bf16[2,6,128,128]{3,2,1,0:T(8,128)(2,1)S(1)}, u32[]{:S(2)}, u32[]{:S(2)}) collective-permute-start(bf16[2,6,128,128]{3,2,1,0:T(8,128)(2,1)S(1)} %get-tuple-element.58), channel_id=1, source_target_pairs={{1,2},{2,1},{3,4},{4,3},{5,6},{6,5},{9,10},{10,9},{11,12},{12,11},... | collective-permute-start | bytes 1179656 | tf_op jit(solution)/shard_map/ppermute | solution.py:320
  112.4 1.7 collective-permute-done.9.far_ref
  114.1 6.4 %half.7.rest_0_ = bf16[16,8,128,128]{3,2,1,0:T(8,128)(2,1)S(1)} custom-call(f32[12,128]{1,0:T(8,128)S(1)} %get-tuple-element.45.w_ref, bf16[4,16,128,128]{3,2,1,0:T(8,128)(2,1)S(1)} %get-tuple-element.63.t_ref.rest_0_, bf16[4,16,128,128]{3,2,1,0:T(8,128)(2,1)S(1)} %get-tuple-element.51.c_ref, bf16[8,16,128,128]{3,2,1,0:T(8,128)(2,1)S(1)} %get-tuple-element.46.k_ref, ...), custom_call_target="tpu_custom_call" | custom-call | flops 1073741824 | bytes 4194304 | tf_op jit(solution)/shard_map/half/pallas_call | solution.py:340
  120.5 3.4 %half.8.rest_0_ = bf16[16,8,128,128]{3,2,1,0:T(8,128)(2,1)S(1)} custom-call(f32[12,128]{1,0:T(8,128)S(1)} %get-tuple-element.45.w_ref, bf16[2,16,128,128]{3,2,1,0:T(8,128)(2,1)S(1)} %get-tuple-element.59.t_ref.rest_1_, bf16[4,16,128,128]{3,2,1,0:T(8,128)(2,1)S(1)} %get-tuple-element.37.c_ref, ...), custom_call_target="tpu_custom_call", output_to_operand_aliasing={{}: (7, {})} | custom-call | flops 536870912 | bytes 4194304 | tf_op jit(solution)/shard_map/half/pallas_call | solution.py:340
  124.0 3.5 %half.9.h_ref = bf16[16,8,128,128]{3,2,1,0:T(8,128)(2,1)S(1)} custom-call(f32[12,128]{1,0:T(8,128)S(1)} %get-tuple-element.45.w_ref, bf16[2,16,128,128]{3,2,1,0:T(8,128)(2,1)S(1)} %get-tuple-element.55.t_ref.rest_2_, bf16[4,16,128,128]{3,2,1,0:T(8,128)(2,1)S(1)} %get-tuple-element.37.c_ref, ...), custom_call_target="tpu_custom_call", output_to_operand_aliasing={{}: (7, {})} | custom-call | flops 536870912 | bytes 4194304 | tf_op jit(solution)/shard_map/half/pallas_call | solution.py:340
  127.5 56.4 %all_to_all.11 = bf16[128,1,128,128]{3,2,1,0:T(8,128)(2,1)S(1)} all-to-all(bf16[128,1,128,128]{3,2,1,0:T(8,128)(2,1)S(1)} %bitcast.12), channel_id=1, replica_groups=mesh['ia'=16,'ja'=8] {'ia','ja'}, dimensions={0} | all-to-all | bytes 8388608 | tf_op jit(solution)/shard_map/all_to_all | solution.py:389
  183.9 3.4 %last.1 = bf16[8,1,16,128,128]{4,3,2,1,0:T(8,128)(2,1)} custom-call(f32[8,16,128,128]{3,2,1,0:T(8,128)S(1)} %get-tuple-element.44.gain_ref, bf16[16,8,128,128]{3,2,1,0:T(8,128)(2,1)S(1)} %half.9.h_ref, bf16[16,8,128,128]{3,2,1,0:T(8,128)(2,1)S(1)} %bitcast.16, bf16[4,16,128,128]{3,2,1,0:T(8,128)(2,1)S(1)} %get-tuple-element.63.t_ref.rest_0_, ...), custom_call_target="tpu_custom_call" | custom-call | bytes 8388608 | tf_op jit(solution)/shard_map/last/pallas_call | solution.py:353
  (12 shorter events, 0.0 us)
Async XLA Ops:
  0.0 8.8 %copy-start.3 = (s32[8,1,16]{2,1,0:T(1,128)S(1)}, s32[8,1,16]{2,1,0:T(1,128)}, u32[]{:S(2)}) copy-start(s32[8,1,16]{2,1,0:T(1,128)} %counts_ref.2) | copy-start | bytes 1540
  4.1 16.6 %collective-permute-start.2 = (bf16[4,6,128,128]{3,2,1,0:T(8,128)(2,1)S(1)}, bf16[4,6,128,128]{3,2,1,0:T(8,128)(2,1)S(1)}, u32[]{:S(2)}, u32[]{:S(2)}) collective-permute-start(bf16[4,6,128,128]{3,2,1,0:T(8,128)(2,1)S(1)} %get-tuple-element.53), channel_id=1, source_target_pairs={{0,1},{1,0},{2,3},{3,2},{4,5},{5,4},{6,7},{7,6},{8,9},{9,8},{10,11... | collective-permute-start | bytes 2359304 | tf_op jit(solution)/shard_map/ppermute | solution.py:321
  5.6 15.1 %collective-permute-start.3 = (bf16[4,6,128,128]{3,2,1,0:T(8,128)(2,1)S(1)}, bf16[4,6,128,128]{3,2,1,0:T(8,128)(2,1)S(1)}, u32[]{:S(2)}, u32[]{:S(2)}) collective-permute-start(bf16[4,6,128,128]{3,2,1,0:T(8,128)(2,1)S(1)} %get-tuple-element.54), channel_id=1, source_target_pairs={{1,2},{2,1},{3,4},{4,3},{5,6},{6,5},{9,10},{10,9},{11,12},{12,11},... | collective-permute-start | bytes 2359304 | tf_op jit(solution)/shard_map/ppermute | solution.py:320
  8.8 7.1 %copy-start = (f32[8,1,16,128]{3,2,1,0:T(8,128)S(1)}, f32[8,1,16,128]{3,2,1,0:T(8,128)}, u32[]{:S(2)}) copy-start(f32[8,1,16,128]{3,2,1,0:T(8,128)} %e_ref) | copy-start | bytes 196612
  8.8 7.1 %copy-start.1 = (f32[128,128]{1,0:T(8,128)S(1)}, f32[128,128]{1,0:T(8,128)}, u32[]{:S(2)}) copy-start(f32[128,128]{1,0:T(8,128)} %fock_ref) | copy-start | bytes 196612
  8.8 7.1 %copy-start.2 = (s32[8,1,16,12]{2,1,3,0:T(1,128)S(1)}, s32[8,1,16,12]{2,1,3,0:T(1,128)}, u32[]{:S(2)}) copy-start(s32[8,1,16,12]{2,1,3,0:T(1,128)} %param.13) | copy-start | bytes 18436
  8.9 7.1 %copy-start.4 = (f32[128]{0:T(128)S(1)}, f32[128]{0:T(128)}, u32[]{:S(2)}) copy-start(f32[128]{0:T(128)} %occ_ref) | copy-start | bytes 1540
  12.3 14.7 %collective-permute-start = (bf16[4,6,128,128]{3,2,1,0:T(8,128)(2,1)S(1)}, bf16[4,6,128,128]{3,2,1,0:T(8,128)(2,1)S(1)}, u32[]{:S(2)}, u32[]{:S(2)}) collective-permute-start(bf16[4,6,128,128]{3,2,1,0:T(8,128)(2,1)S(1)} %get-tuple-element.48), channel_id=1, source_target_pairs={{0,1},{1,0},{2,3},{3,2},{4,5},{5,4},{6,7},{7,6},{8,9},{9,8},{10,11... | collective-permute-start | bytes 2359304 | tf_op jit(solution)/shard_map/ppermute | solution.py:321
  12.4 15.0 %collective-permute-start.1 = (bf16[4,6,128,128]{3,2,1,0:T(8,128)(2,1)S(1)}, bf16[4,6,128,128]{3,2,1,0:T(8,128)(2,1)S(1)}, u32[]{:S(2)}, u32[]{:S(2)}) collective-permute-start(bf16[4,6,128,128]{3,2,1,0:T(8,128)(2,1)S(1)} %get-tuple-element.49), channel_id=1, source_target_pairs={{1,2},{2,1},{3,4},{4,3},{5,6},{6,5},{9,10},{10,9},{11,12},{12,11},... | collective-permute-start | bytes 2359304 | tf_op jit(solution)/shard_map/ppermute | solution.py:320
  99.9 9.8 %collective-permute-start.8 = (bf16[4,6,128,128]{3,2,1,0:T(8,128)(2,1)S(1)}, bf16[4,6,128,128]{3,2,1,0:T(8,128)(2,1)S(1)}, u32[]{:S(2)}, u32[]{:S(2)}) collective-permute-start(bf16[4,6,128,128]{3,2,1,0:T(8,128)(2,1)S(1)} %get-tuple-element.65), channel_id=1, source_target_pairs={{0,1},{1,0},{2,3},{3,2},{4,5},{5,4},{6,7},{7,6},{8,9},{9,8},{10,11... | collective-permute-start | bytes 2359304 | tf_op jit(solution)/shard_map/ppermute | solution.py:321
  100.8 13.3 %collective-permute-start.9 = (bf16[4,6,128,128]{3,2,1,0:T(8,128)(2,1)S(1)}, bf16[4,6,128,128]{3,2,1,0:T(8,128)(2,1)S(1)}, u32[]{:S(2)}, u32[]{:S(2)}) collective-permute-start(bf16[4,6,128,128]{3,2,1,0:T(8,128)(2,1)S(1)} %get-tuple-element.66), channel_id=1, source_target_pairs={{1,2},{2,1},{3,4},{4,3},{5,6},{6,5},{9,10},{10,9},{11,12},{12,11},... | collective-permute-start | bytes 2359304 | tf_op jit(solution)/shard_map/ppermute | solution.py:320
  104.4 16.1 %collective-permute-start.6 = (bf16[2,6,128,128]{3,2,1,0:T(8,128)(2,1)S(1)}, bf16[2,6,128,128]{3,2,1,0:T(8,128)(2,1)S(1)}, u32[]{:S(2)}, u32[]{:S(2)}) collective-permute-start(bf16[2,6,128,128]{3,2,1,0:T(8,128)(2,1)S(1)} %get-tuple-element.61), channel_id=1, source_target_pairs={{0,1},{1,0},{2,3},{3,2},{4,5},{5,4},{6,7},{7,6},{8,9},{9,8},{10,11... | collective-permute-start | bytes 1179656 | tf_op jit(solution)/shard_map/ppermute | solution.py:321
  104.5 16.0 %collective-permute-start.7 = (bf16[2,6,128,128]{3,2,1,0:T(8,128)(2,1)S(1)}, bf16[2,6,128,128]{3,2,1,0:T(8,128)(2,1)S(1)}, u32[]{:S(2)}, u32[]{:S(2)}) collective-permute-start(bf16[2,6,128,128]{3,2,1,0:T(8,128)(2,1)S(1)} %get-tuple-element.62), channel_id=1, source_target_pairs={{1,2},{2,1},{3,4},{4,3},{5,6},{6,5},{9,10},{10,9},{11,12},{12,11},... | collective-permute-start | bytes 1179656 | tf_op jit(solution)/shard_map/ppermute | solution.py:320
  109.6 14.3 %collective-permute-start.4 = (bf16[2,6,128,128]{3,2,1,0:T(8,128)(2,1)S(1)}, bf16[2,6,128,128]{3,2,1,0:T(8,128)(2,1)S(1)}, u32[]{:S(2)}, u32[]{:S(2)}) collective-permute-start(bf16[2,6,128,128]{3,2,1,0:T(8,128)(2,1)S(1)} %get-tuple-element.57), channel_id=1, source_target_pairs={{0,1},{1,0},{2,3},{3,2},{4,5},{5,4},{6,7},{7,6},{8,9},{9,8},{10,11... | collective-permute-start | bytes 1179656 | tf_op jit(solution)/shard_map/ppermute | solution.py:321
  109.7 14.2 %collective-permute-start.5 = (bf16[2,6,128,128]{3,2,1,0:T(8,128)(2,1)S(1)}, bf16[2,6,128,128]{3,2,1,0:T(8,128)(2,1)S(1)}, u32[]{:S(2)}, u32[]{:S(2)}) collective-permute-start(bf16[2,6,128,128]{3,2,1,0:T(8,128)(2,1)S(1)} %get-tuple-element.58), channel_id=1, source_target_pairs={{1,2},{2,1},{3,4},{4,3},{5,6},{6,5},{9,10},{10,9},{11,12},{12,11},... | collective-permute-start | bytes 1179656 | tf_op jit(solution)/shard_map/ppermute | solution.py:320

commit v5 on v4

--- a/solution.py
+++ b/solution.py
@@ -11,7 +11,7 @@
 ITERS = 2
 DAMPING = 0.5
 GROUPS = ((4, 4), (4, 2, 2))
-SKEW = 4
+SKEW = 6
 VMEM_BYTES = 16 * 1024 * 1024
 
 BF = jnp.bfloat16

time: 188 us -> 188 us (level)
  transfers between devices with their start and end apart: 10 -> 10, of which waited for: 2 -> 2; matrix products, arithmetic and copies ran while one was open for 0% -> 0% of each run, Pallas kernels for 15% -> 14%
where the time goes in v5:
time: 188 us; the launch traced here: 187 us
  blocking collectives  120 us (64%)
  Pallas kernels  47.3 us (25%)
  starting transfers between devices  17.7 us (9%)
  waiting for transfers between devices  2.33 us (1%)
    all_to_all x2, blocking collectives, on_device(): lax.all_to_all(sent, ('ia', 'ja'), split_axis=0, concat_axis=0, tiled=True)  120 us
    pallas_call x5, Pallas kernels, half_step(): pl.pallas_call(partial(half_kernel, offset, offset % size), in_specs=[SME...  25.9 us
    ppermute x5, starting transfers between devices, exchange(): from_far = lax.ppermute(made[2], 'ja', far_pairs)  15 us
    pallas_call x3, Pallas kernels, next_step(): pl.pallas_call(partial(middle_kernel, offset, offset % size), in_specs=[V...  6.01 us
    pallas_call x1, Pallas kernels, first_steps(): pl.pallas_call(gain_kernel, in_specs=[SMEM] * 2 + [VMEM] * 3, out_shape=[...  4.72 us
    pallas_call x1, Pallas kernels, first_steps(): pl.pallas_call(start_kernel, in_specs=[HBM, HBM, HBM], out_shape=[group]...  3.97 us
  transfers between devices with their start and end apart: 10, of which 2 were waited for; matrix products, arithmetic and copies ran while one was open for 0% of the time, Pallas kernels for 14%

profile of v5, /device:TPU:1, one launch (start us, length us, event | category | flops | bytes accessed | tf_op | source)
XLA Modules:
  0.0 187.2 jit_solution(1452408525788323477)
XLA Ops:
  0.0 4.0 %start.1 = (bf16[4,16,128,128]{3,2,1,0:T(8,128)(2,1)S(1)}, bf16[4,16,128,128]{3,2,1,0:T(8,128)(2,1)S(1)}, bf16[4,16,128,128]{3,2,1,0:T(8,128)(2,1)S(1)}, bf16[4,...) custom-call(s32[8,1,16]{2,1,0:T(1,128)} %counts_ref.2, ...), custom_call_target="tpu_custom_call" | custom-call | flops 536870912 | bytes 8388608 | tf_op jit(solution)/shard_map/start/pallas_call | solution.py:278
  4.0 1.5 collective-permute-start.2
  5.5 3.2 %collective-permute-start.3 = (bf16[4,6,128,128]{3,2,1,0:T(8,128)(2,1)S(1)}, bf16[4,6,128,128]{3,2,1,0:T(8,128)(2,1)S(1)}, u32[]{:S(2)}, u32[]{:S(2)}) collective-permute-start(bf16[4,6,128,128]{3,2,1,0:T(8,128)(2,1)S(1)} %get-tuple-element.54), channel_id=1, source_target_pairs={{1,2},{2,1},{3,4},{4,3},{5,6},{6,5},{9,10},{10,9},{11,12},{12,11},... | collective-permute-start | bytes 2359304 | tf_op jit(solution)/shard_map/ppermute | solution.py:320
  8.7 0.0 copy-start
  8.7 0.0 copy-start.1
  8.7 0.0 copy-start.2
  8.7 0.0 copy-start.4
  8.7 3.3 %second.1 = (bf16[4,16,128,128]{3,2,1,0:T(8,128)(2,1)S(1)}, bf16[8,16,128,128]{3,2,1,0:T(8,128)(2,1)S(1)}, bf16[4,16,128,128]{3,2,1,0:T(8,128)(2,1)S(1)}, bf16[4...) custom-call(s32[8,1,16]{2,1,0:T(1,128)S(1)} %copy-done.3, ...), custom_call_target="tpu_custom_call" | custom-call | flops 536870912 | bytes 4194304 | tf_op jit(solution)/shard_map/second/pallas_call | solution.py:294
  12.0 0.1 collective-permute-start
  12.1 3.6 %collective-permute-start.1 = (bf16[4,6,128,128]{3,2,1,0:T(8,128)(2,1)S(1)}, bf16[4,6,128,128]{3,2,1,0:T(8,128)(2,1)S(1)}, u32[]{:S(2)}, u32[]{:S(2)}) collective-permute-start(bf16[4,6,128,128]{3,2,1,0:T(8,128)(2,1)S(1)} %get-tuple-element.49), channel_id=1, source_target_pairs={{1,2},{2,1},{3,4},{4,3},{5,6},{6,5},{9,10},{10,9},{11,12},{12,11},... | collective-permute-start | bytes 2359304 | tf_op jit(solution)/shard_map/ppermute | solution.py:320
  15.7 4.7 %gain.1 = (f32[8,16,128,128]{3,2,1,0:T(8,128)S(1)}, f32[12,128]{1,0:T(8,128)S(1)}) custom-call(f32[128]{0:T(128)S(1)} %copy-done.4, s32[8,1,16]{2,1,0:T(1,128)S(1)} %copy-done.3, f32[8,1,16,128]{3,2,1,0:T(8,128)S(1)} %copy-done, s32[96,1,16]{2,1,0:T(1,128)S(1)} %bitcast.17, f32[128,128]{1,0:T(8,128)S(1)} %copy-done.1), custom_call_target="tpu_custom_call" | custom-call | flops 16777216 | bytes 8388608 | tf_op jit(solution)/shard_map/gain/pallas_call | solution.py:305
  20.5 0.0 collective-permute-done.3.far_ref
  20.5 6.2 %half.5.rest_0_ = bf16[16,8,128,128]{3,2,1,0:T(8,128)(2,1)S(1)} custom-call(f32[12,128]{1,0:T(8,128)S(1)} %get-tuple-element.45.w_ref, bf16[4,16,128,128]{3,2,1,0:T(8,128)(2,1)S(1)} %get-tuple-element.50.t_ref, bf16[4,16,128,128]{3,2,1,0:T(8,128)(2,1)S(1)} %get-tuple-element.51.c_ref, bf16[8,16,128,128]{3,2,1,0:T(8,128)(2,1)S(1)} %get-tuple-element.46.k_ref, ...), custom_call_target="tpu_custom_call" | custom-call | flops 1073741824 | bytes 4194304 | tf_op jit(solution)/shard_map/half/pallas_call | solution.py:340
  26.7 0.5 collective-permute-done.1.far_ref
  27.2 6.3 %half.6.h_ref = bf16[16,8,128,128]{3,2,1,0:T(8,128)(2,1)S(1)} custom-call(f32[12,128]{1,0:T(8,128)S(1)} %get-tuple-element.45.w_ref, bf16[4,16,128,128]{3,2,1,0:T(8,128)(2,1)S(1)} %get-tuple-element.38.t_ref, bf16[4,16,128,128]{3,2,1,0:T(8,128)(2,1)S(1)} %get-tuple-element.37.c_ref, ...), custom_call_target="tpu_custom_call", output_to_operand_aliasing={{}: (7, {})} | custom-call | flops 1073741824 | bytes 4194304 | tf_op jit(solution)/shard_map/half/pallas_call | solution.py:340
  33.6 63.2 %all_to_all.10 = bf16[128,1,128,128]{3,2,1,0:T(8,128)(2,1)S(1)} all-to-all(bf16[128,1,128,128]{3,2,1,0:T(8,128)(2,1)S(1)} %bitcast.11), channel_id=1, replica_groups=mesh['ia'=16,'ja'=8] {'ia','ja'}, dimensions={0} | all-to-all | bytes 8388608 | tf_op jit(solution)/shard_map/all_to_all | solution.py:389
  96.7 3.0 %middle.5 = (bf16[4,16,128,128]{3,2,1,0:T(8,128)(2,1)S(1)}, bf16[4,16,128,128]{3,2,1,0:T(8,128)(2,1)S(1)}, bf16[4,6,128,128]{3,2,1,0:T(8,128)(2,1)S(1)}, bf16[4,6,128,128]{3,2,1,0:T(8,128)(2,1)S(1)}) custom-call(f32[8,16,128,128]{3,2,1,0:T(8,128)S(1)} %get-tuple-element.44.gain_ref, bf16[16,8,128,128]{3,2,1,0:T(8,128)(2,1)S(1)} %half.6.h_ref, ...), custom_call_target="tpu_custom_call" | custom-call | flops 536870912 | bytes 2097152 | tf_op jit(solution)/shard_map/middle/pallas_call | solution.py:324
  99.7 0.9 collective-permute-start.8
  100.6 2.0 %collective-permute-start.9 = (bf16[4,6,128,128]{3,2,1,0:T(8,128)(2,1)S(1)}, bf16[4,6,128,128]{3,2,1,0:T(8,128)(2,1)S(1)}, u32[]{:S(2)}, u32[]{:S(2)}) collective-permute-start(bf16[4,6,128,128]{3,2,1,0:T(8,128)(2,1)S(1)} %get-tuple-element.66), channel_id=1, source_target_pairs={{1,2},{2,1},{3,4},{4,3},{5,6},{6,5},{9,10},{10,9},{11,12},{12,11},... | collective-permute-start | bytes 2359304 | tf_op jit(solution)/shard_map/ppermute | solution.py:320
  102.6 1.5 middle.4
  104.2 0.1 collective-permute-start.6
  104.3 3.5 %collective-permute-start.7 = (bf16[2,6,128,128]{3,2,1,0:T(8,128)(2,1)S(1)}, bf16[2,6,128,128]{3,2,1,0:T(8,128)(2,1)S(1)}, u32[]{:S(2)}, u32[]{:S(2)}) collective-permute-start(bf16[2,6,128,128]{3,2,1,0:T(8,128)(2,1)S(1)} %get-tuple-element.62), channel_id=1, source_target_pairs={{1,2},{2,1},{3,4},{4,3},{5,6},{6,5},{9,10},{10,9},{11,12},{12,11},... | collective-permute-start | bytes 1179656 | tf_op jit(solution)/shard_map/ppermute | solution.py:320
  107.8 1.5 middle.3
  109.3 0.1 collective-permute-start.4
  109.4 2.7 %collective-permute-start.5 = (bf16[2,6,128,128]{3,2,1,0:T(8,128)(2,1)S(1)}, bf16[2,6,128,128]{3,2,1,0:T(8,128)(2,1)S(1)}, u32[]{:S(2)}, u32[]{:S(2)}) collective-permute-start(bf16[2,6,128,128]{3,2,1,0:T(8,128)(2,1)S(1)} %get-tuple-element.58), channel_id=1, source_target_pairs={{1,2},{2,1},{3,4},{4,3},{5,6},{6,5},{9,10},{10,9},{11,12},{12,11},... | collective-permute-start | bytes 1179656 | tf_op jit(solution)/shard_map/ppermute | solution.py:320
  112.1 1.8 collective-permute-done.9.far_ref
  113.9 6.4 %half.7.rest_0_ = bf16[16,8,128,128]{3,2,1,0:T(8,128)(2,1)S(1)} custom-call(f32[12,128]{1,0:T(8,128)S(1)} %get-tuple-element.45.w_ref, bf16[4,16,128,128]{3,2,1,0:T(8,128)(2,1)S(1)} %get-tuple-element.63.t_ref.rest_0_, bf16[4,16,128,128]{3,2,1,0:T(8,128)(2,1)S(1)} %get-tuple-element.51.c_ref, bf16[8,16,128,128]{3,2,1,0:T(8,128)(2,1)S(1)} %get-tuple-element.46.k_ref, ...), custom_call_target="tpu_custom_call" | custom-call | flops 1073741824 | bytes 4194304 | tf_op jit(solution)/shard_map/half/pallas_call | solution.py:340
  120.3 0.0 collective-permute-done.6.near_ref
  120.3 3.4 %half.8.rest_0_ = bf16[16,8,128,128]{3,2,1,0:T(8,128)(2,1)S(1)} custom-call(f32[12,128]{1,0:T(8,128)S(1)} %get-tuple-element.45.w_ref, bf16[2,16,128,128]{3,2,1,0:T(8,128)(2,1)S(1)} %get-tuple-element.59.t_ref.rest_1_, bf16[4,16,128,128]{3,2,1,0:T(8,128)(2,1)S(1)} %get-tuple-element.37.c_ref, ...), custom_call_target="tpu_custom_call", output_to_operand_aliasing={{}: (7, {})} | custom-call | flops 536870912 | bytes 4194304 | tf_op jit(solution)/shard_map/half/pallas_call | solution.py:340
  123.8 3.5 %half.9.h_ref = bf16[16,8,128,128]{3,2,1,0:T(8,128)(2,1)S(1)} custom-call(f32[12,128]{1,0:T(8,128)S(1)} %get-tuple-element.45.w_ref, bf16[2,16,128,128]{3,2,1,0:T(8,128)(2,1)S(1)} %get-tuple-element.55.t_ref.rest_2_, bf16[4,16,128,128]{3,2,1,0:T(8,128)(2,1)S(1)} %get-tuple-element.37.c_ref, ...), custom_call_target="tpu_custom_call", output_to_operand_aliasing={{}: (7, {})} | custom-call | flops 536870912 | bytes 4194304 | tf_op jit(solution)/shard_map/half/pallas_call | solution.py:340
  127.3 56.4 %all_to_all.11 = bf16[128,1,128,128]{3,2,1,0:T(8,128)(2,1)S(1)} all-to-all(bf16[128,1,128,128]{3,2,1,0:T(8,128)(2,1)S(1)} %bitcast.12), channel_id=1, replica_groups=mesh['ia'=16,'ja'=8] {'ia','ja'}, dimensions={0} | all-to-all | bytes 8388608 | tf_op jit(solution)/shard_map/all_to_all | solution.py:389
  183.7 3.4 %last.1 = bf16[8,1,16,128,128]{4,3,2,1,0:T(8,128)(2,1)} custom-call(f32[8,16,128,128]{3,2,1,0:T(8,128)S(1)} %get-tuple-element.44.gain_ref, bf16[16,8,128,128]{3,2,1,0:T(8,128)(2,1)S(1)} %half.9.h_ref, bf16[16,8,128,128]{3,2,1,0:T(8,128)(2,1)S(1)} %bitcast.16, bf16[4,16,128,128]{3,2,1,0:T(8,128)(2,1)S(1)} %get-tuple-element.63.t_ref.rest_0_, ...), custom_call_target="tpu_custom_call" | custom-call | bytes 8388608 | tf_op jit(solution)/shard_map/last/pallas_call | solution.py:353
  (12 shorter events, 0.0 us)
Async XLA Ops:
  0.0 8.7 %copy-start.3 = (s32[8,1,16]{2,1,0:T(1,128)S(1)}, s32[8,1,16]{2,1,0:T(1,128)}, u32[]{:S(2)}) copy-start(s32[8,1,16]{2,1,0:T(1,128)} %counts_ref.2) | copy-start | bytes 1540
  4.0 16.5 %collective-permute-start.2 = (bf16[4,6,128,128]{3,2,1,0:T(8,128)(2,1)S(1)}, bf16[4,6,128,128]{3,2,1,0:T(8,128)(2,1)S(1)}, u32[]{:S(2)}, u32[]{:S(2)}) collective-permute-start(bf16[4,6,128,128]{3,2,1,0:T(8,128)(2,1)S(1)} %get-tuple-element.53), channel_id=1, source_target_pairs={{0,1},{1,0},{2,3},{3,2},{4,5},{5,4},{6,7},{7,6},{8,9},{9,8},{10,11... | collective-permute-start | bytes 2359304 | tf_op jit(solution)/shard_map/ppermute | solution.py:321
  5.5 15.0 %collective-permute-start.3 = (bf16[4,6,128,128]{3,2,1,0:T(8,128)(2,1)S(1)}, bf16[4,6,128,128]{3,2,1,0:T(8,128)(2,1)S(1)}, u32[]{:S(2)}, u32[]{:S(2)}) collective-permute-start(bf16[4,6,128,128]{3,2,1,0:T(8,128)(2,1)S(1)} %get-tuple-element.54), channel_id=1, source_target_pairs={{1,2},{2,1},{3,4},{4,3},{5,6},{6,5},{9,10},{10,9},{11,12},{12,11},... | collective-permute-start | bytes 2359304 | tf_op jit(solution)/shard_map/ppermute | solution.py:320
  8.7 7.0 %copy-start = (f32[8,1,16,128]{3,2,1,0:T(8,128)S(1)}, f32[8,1,16,128]{3,2,1,0:T(8,128)}, u32[]{:S(2)}) copy-start(f32[8,1,16,128]{3,2,1,0:T(8,128)} %e_ref) | copy-start | bytes 196612
  8.7 7.0 %copy-start.1 = (f32[128,128]{1,0:T(8,128)S(1)}, f32[128,128]{1,0:T(8,128)}, u32[]{:S(2)}) copy-start(f32[128,128]{1,0:T(8,128)} %fock_ref) | copy-start | bytes 196612
  8.7 7.0 %copy-start.2 = (s32[8,1,16,12]{2,1,3,0:T(1,128)S(1)}, s32[8,1,16,12]{2,1,3,0:T(1,128)}, u32[]{:S(2)}) copy-start(s32[8,1,16,12]{2,1,3,0:T(1,128)} %param.13) | copy-start | bytes 18436
  8.7 7.0 %copy-start.4 = (f32[128]{0:T(128)S(1)}, f32[128]{0:T(128)}, u32[]{:S(2)}) copy-start(f32[128]{0:T(128)} %occ_ref) | copy-start | bytes 1540
  12.0 14.7 %collective-permute-start = (bf16[4,6,128,128]{3,2,1,0:T(8,128)(2,1)S(1)}, bf16[4,6,128,128]{3,2,1,0:T(8,128)(2,1)S(1)}, u32[]{:S(2)}, u32[]{:S(2)}) collective-permute-start(bf16[4,6,128,128]{3,2,1,0:T(8,128)(2,1)S(1)} %get-tuple-element.48), channel_id=1, source_target_pairs={{0,1},{1,0},{2,3},{3,2},{4,5},{5,4},{6,7},{7,6},{8,9},{9,8},{10,11... | collective-permute-start | bytes 2359304 | tf_op jit(solution)/shard_map/ppermute | solution.py:321
  12.1 15.1 %collective-permute-start.1 = (bf16[4,6,128,128]{3,2,1,0:T(8,128)(2,1)S(1)}, bf16[4,6,128,128]{3,2,1,0:T(8,128)(2,1)S(1)}, u32[]{:S(2)}, u32[]{:S(2)}) collective-permute-start(bf16[4,6,128,128]{3,2,1,0:T(8,128)(2,1)S(1)} %get-tuple-element.49), channel_id=1, source_target_pairs={{1,2},{2,1},{3,4},{4,3},{5,6},{6,5},{9,10},{10,9},{11,12},{12,11},... | collective-permute-start | bytes 2359304 | tf_op jit(solution)/shard_map/ppermute | solution.py:320
  99.7 9.7 %collective-permute-start.8 = (bf16[4,6,128,128]{3,2,1,0:T(8,128)(2,1)S(1)}, bf16[4,6,128,128]{3,2,1,0:T(8,128)(2,1)S(1)}, u32[]{:S(2)}, u32[]{:S(2)}) collective-permute-start(bf16[4,6,128,128]{3,2,1,0:T(8,128)(2,1)S(1)} %get-tuple-element.65), channel_id=1, source_target_pairs={{0,1},{1,0},{2,3},{3,2},{4,5},{5,4},{6,7},{7,6},{8,9},{9,8},{10,11... | collective-permute-start | bytes 2359304 | tf_op jit(solution)/shard_map/ppermute | solution.py:321
  100.6 13.3 %collective-permute-start.9 = (bf16[4,6,128,128]{3,2,1,0:T(8,128)(2,1)S(1)}, bf16[4,6,128,128]{3,2,1,0:T(8,128)(2,1)S(1)}, u32[]{:S(2)}, u32[]{:S(2)}) collective-permute-start(bf16[4,6,128,128]{3,2,1,0:T(8,128)(2,1)S(1)} %get-tuple-element.66), channel_id=1, source_target_pairs={{1,2},{2,1},{3,4},{4,3},{5,6},{6,5},{9,10},{10,9},{11,12},{12,11},... | collective-permute-start | bytes 2359304 | tf_op jit(solution)/shard_map/ppermute | solution.py:320
  104.2 16.1 %collective-permute-start.6 = (bf16[2,6,128,128]{3,2,1,0:T(8,128)(2,1)S(1)}, bf16[2,6,128,128]{3,2,1,0:T(8,128)(2,1)S(1)}, u32[]{:S(2)}, u32[]{:S(2)}) collective-permute-start(bf16[2,6,128,128]{3,2,1,0:T(8,128)(2,1)S(1)} %get-tuple-element.61), channel_id=1, source_target_pairs={{0,1},{1,0},{2,3},{3,2},{4,5},{5,4},{6,7},{7,6},{8,9},{9,8},{10,11... | collective-permute-start | bytes 1179656 | tf_op jit(solution)/shard_map/ppermute | solution.py:321
  104.3 16.0 %collective-permute-start.7 = (bf16[2,6,128,128]{3,2,1,0:T(8,128)(2,1)S(1)}, bf16[2,6,128,128]{3,2,1,0:T(8,128)(2,1)S(1)}, u32[]{:S(2)}, u32[]{:S(2)}) collective-permute-start(bf16[2,6,128,128]{3,2,1,0:T(8,128)(2,1)S(1)} %get-tuple-element.62), channel_id=1, source_target_pairs={{1,2},{2,1},{3,4},{4,3},{5,6},{6,5},{9,10},{10,9},{11,12},{12,11},... | collective-permute-start | bytes 1179656 | tf_op jit(solution)/shard_map/ppermute | solution.py:320
  109.3 14.4 %collective-permute-start.4 = (bf16[2,6,128,128]{3,2,1,0:T(8,128)(2,1)S(1)}, bf16[2,6,128,128]{3,2,1,0:T(8,128)(2,1)S(1)}, u32[]{:S(2)}, u32[]{:S(2)}) collective-permute-start(bf16[2,6,128,128]{3,2,1,0:T(8,128)(2,1)S(1)} %get-tuple-element.57), channel_id=1, source_target_pairs={{0,1},{1,0},{2,3},{3,2},{4,5},{5,4},{6,7},{7,6},{8,9},{9,8},{10,11... | collective-permute-start | bytes 1179656 | tf_op jit(solution)/shard_map/ppermute | solution.py:321
  109.4 14.3 %collective-permute-start.5 = (bf16[2,6,128,128]{3,2,1,0:T(8,128)(2,1)S(1)}, bf16[2,6,128,128]{3,2,1,0:T(8,128)(2,1)S(1)}, u32[]{:S(2)}, u32[]{:S(2)}) collective-permute-start(bf16[2,6,128,128]{3,2,1,0:T(8,128)(2,1)S(1)} %get-tuple-element.58), channel_id=1, source_target_pairs={{1,2},{2,1},{3,4},{4,3},{5,6},{6,5},{9,10},{10,9},{11,12},{12,11},... | collective-permute-start | bytes 1179656 | tf_op jit(solution)/shard_map/ppermute | solution.py:320
